TPU v7x, 32 devices: a whole 2x2x4 slice. The times are simulated.
32 devices in a mesh: dp: 2 (over x), seq: 4 (over y, core), fsdp: 4 (over z).
Axes of the slice: x: 2, y: 2, z: 4, core: 2. Of those that a mesh axis runs over, the one named last changes fastest.
Arguments:
- tokens: bfloat16 [8, 1024, 1024], P(('dp', 'fsdp'), 'seq'), may hold values from -6 to 6
- out_grad: bfloat16 [8, 1024, 1024], P(('dp', 'fsdp'), 'seq'), may hold values from -6 to 6
- doc_lengths: int32 [8, 4], P(('dp', 'fsdp')), may hold values from 1 to 896, as said below
- positions: int32 [8, 1024], P(('dp', 'fsdp'), 'seq'), may hold values from 0 to 2685, as said below
- norm1_gain: bfloat16 [1024], P(('dp', 'seq', 'fsdp')), may hold values from 0.5 to 1.5
- w_query: bfloat16 [1024, 1024], P(('dp', 'seq', 'fsdp')), may hold values from -0.1875 to 0.1875
- key_weight: bfloat16 [1024, 512], P(('dp', 'seq', 'fsdp')), may hold values from -0.1875 to 0.1875
- value_weight: bfloat16 [1024, 512], P(('dp', 'seq', 'fsdp')), may hold values from -0.1875 to 0.1875
- w_out: bfloat16 [1024, 1024], P(('dp', 'seq', 'fsdp')), may hold values from -3 to 3
- q_gain: bfloat16 [64], replicated, may hold values from 0.25 to 1.75
- k_gain: bfloat16 [64], replicated, may hold values from 0.25 to 1.75
- norm2_gain: bfloat16 [1024], P(('dp', 'seq', 'fsdp')), may hold values from 0.5 to 1.5
- w_gate: bfloat16 [1024, 4608], P(('dp', 'seq', 'fsdp')), may hold values from -0.1875 to 0.1875
- w_up: bfloat16 [1024, 4608], P(('dp', 'seq', 'fsdp')), may hold values from -0.1875 to 0.1875
- w_down: bfloat16 [4608, 1024], P(('dp', 'seq', 'fsdp')), may hold values from -0.09375 to 0.09375
Outputs:
- block_out: bfloat16 [8, 1024, 1024], P(('dp', 'fsdp'), 'seq')
- input_grad: bfloat16 [8, 1024, 1024], P(('dp', 'fsdp'), 'seq')
- grad_norm1: float32 [1024], P(('dp', 'seq', 'fsdp'))
- grad_query: float32 [1024, 1024], P(('dp', 'seq', 'fsdp'))
- grad_key: float32 [1024, 512], P(('dp', 'seq', 'fsdp'))
- grad_value: float32 [1024, 512], P(('dp', 'seq', 'fsdp'))
- grad_out: float32 [1024, 1024], P(('dp', 'seq', 'fsdp'))
- grad_q_gain: float32 [64], replicated
- grad_k_gain: float32 [64], replicated
- grad_norm2: float32 [1024], P(('dp', 'seq', 'fsdp'))
- grad_gate: float32 [1024, 4608], P(('dp', 'seq', 'fsdp'))
- grad_up: float32 [1024, 4608], P(('dp', 'seq', 'fsdp'))
- grad_down: float32 [4608, 1024], P(('dp', 'seq', 'fsdp'))
Inputs may be any that keep to these rules, and one draw needn't show every extreme that they name: `doc_lengths`: each sequence holds 4 documents, in order, whose lengths sum to 1024; the longest has exactly 896 tokens. `positions`: positions start at 0 at each document's first token and rise by a fixed step of 1 to 3 per token within a document; the longest document's step is 3.
All inputs are finite; a program needn't handle non-finite values.
Results may differ from a plain program's by a relative error of at most 0.019.
Values may be sent and summed in bfloat16 or wider, within the bound.
A program may use at most 256 MiB of HBM per device.

v0:
```python
import jax
import jax.numpy as jnp
from jax import lax
from jax.sharding import PartitionSpec as P

MODEL_WIDTH = 1024
QUERY_HEADS = 16
KEY_VALUE_HEADS = 8
HEAD_SIZE = 64
FF = 4608


epsilon = 1e-05
rope_base = 1000000.0
score_scale = 0.125
masked_fill_value = -1e30


def rms_scale(value_rows, norm_gain):
    return (
        value_rows
        * lax.rsqrt(jnp.mean(value_rows * value_rows, axis=-1, keepdims=True) + epsilon)
        * norm_gain
    )


def rotary_tables(position):
    half_width = HEAD_SIZE // 2
    freqs = rope_base ** (-2.0 * jnp.arange(half_width, dtype=jnp.float32) / HEAD_SIZE)
    angles = position.astype(jnp.float32)[:, None] * freqs[None, :]
    angles = jnp.concatenate([angles, angles], axis=1)
    return (jnp.cos(angles), jnp.sin(angles))


def head_norm_rotary(unnormed_rows, norm_gain, cosine_table, sine_table, heads):
    token_rows = unnormed_rows.shape[0]
    split_rows = unnormed_rows.reshape(token_rows, heads, HEAD_SIZE)
    normed = rms_scale(split_rows, norm_gain)
    first_half = normed[..., : HEAD_SIZE // 2]
    second_half = normed[..., HEAD_SIZE // 2 :]
    turned = jnp.concatenate([-second_half, first_half], axis=-1)
    rotated = normed * cosine_table[:, None, :] + turned * sine_table[:, None, :]
    return rotated.reshape(token_rows, heads * HEAD_SIZE)


def segment_ids(lengths, length_all):
    doc_ends = jnp.cumsum(lengths)
    indices = jnp.arange(length_all, dtype=jnp.int32)
    return jnp.sum((indices[:, None] >= doc_ends[None, :]).astype(jnp.int32), axis=1)


def rounded(value_rows):
    return lax.optimization_barrier(value_rows.astype(jnp.bfloat16)).astype(jnp.float32)


def matmul(left, right):
    return jnp.dot(left, right, preferred_element_type=jnp.float32)


def contract_rows(left, right):
    return lax.dot_general(
        left, right, (((0,), (0,)), ((), ())), preferred_element_type=jnp.float32
    )


def contract_cols(left, right):
    return lax.dot_general(
        left, right, (((1,), (1,)), ((), ())), preferred_element_type=jnp.float32
    )


def column_term(left, right):
    return contract_rows(left, right)


def body(
    tokens,
    out_grad,
    doc_lengths,
    positions,
    norm1_gain,
    w_query,
    key_weight,
    value_weight,
    w_out,
    q_gain,
    k_gain,
    norm2_gain,
    w_gate,
    w_up,
    w_down,
):
    token_rows = tokens.shape[1]
    seq_parts = lax.axis_size("seq")
    my_index = lax.axis_index("seq")
    seq_len = token_rows * seq_parts
    queries_per_group = QUERY_HEADS // KEY_VALUE_HEADS
    segments = segment_ids(doc_lengths[0], seq_len)
    own_offset = my_index * token_rows
    own_segments = lax.dynamic_slice_in_dim(segments, own_offset, token_rows)
    own_places = own_offset + jnp.arange(token_rows, dtype=jnp.int32)
    cosine_table, sine_table = rotary_tables(positions[0])
    norm1_all, query_all, key_all, value_all, out_all = (
        lax.all_gather(norm1_gain, ("dp", "seq", "fsdp"), axis=0, tiled=True),
        lax.all_gather(w_query, ("dp", "seq", "fsdp"), axis=0, tiled=True),
        lax.all_gather(key_weight, ("dp", "seq", "fsdp"), axis=0, tiled=True),
        lax.all_gather(value_weight, ("dp", "seq", "fsdp"), axis=0, tiled=True),
        lax.all_gather(w_out, ("dp", "seq", "fsdp"), axis=0, tiled=True),
    )
    inputs = tokens[0].astype(jnp.float32)
    gain_one = norm1_all.astype(jnp.float32)
    normed1 = rms_scale(inputs, gain_one).astype(jnp.bfloat16)
    query_raw = matmul(normed1, query_all)
    key_unnormed = matmul(normed1, key_all)
    value_raw = matmul(normed1, value_all)
    gain_query = q_gain.astype(jnp.float32)
    gain_key = k_gain.astype(jnp.float32)

    def query_part(unnormed_rows, norm_gain):
        return head_norm_rotary(unnormed_rows, norm_gain, cosine_table, sine_table, QUERY_HEADS)

    def key_part(unnormed_rows, norm_gain):
        return head_norm_rotary(unnormed_rows, norm_gain, cosine_table, sine_table, KEY_VALUE_HEADS)

    query_rows = query_part(query_raw, gain_query).astype(jnp.bfloat16)
    key_rows = key_part(key_unnormed, gain_key).astype(jnp.bfloat16)
    value_rows = value_raw.astype(jnp.bfloat16)
    query_four_axes = query_rows.reshape(token_rows, KEY_VALUE_HEADS, queries_per_group, HEAD_SIZE)

    def scores_for(key_rows_part):
        total_amount = key_rows_part.shape[0]
        key_three_axes = key_rows_part.reshape(total_amount, KEY_VALUE_HEADS, HEAD_SIZE)
        scores = (
            jnp.einsum(
                "qhgd,khd->hgqk",
                query_four_axes,
                key_three_axes,
                preferred_element_type=jnp.float32,
            )
            * score_scale
        )
        key_places = jnp.arange(total_amount, dtype=jnp.int32)
        allowed = (own_segments[:, None] == segments[None, :]) & (
            own_places[:, None] >= key_places[None, :]
        )
        return (scores, allowed, key_three_axes)

    starting_maximum = jnp.full(
        (KEY_VALUE_HEADS, queries_per_group, token_rows), masked_fill_value, jnp.float32
    )
    row_top = starting_maximum
    key_rows_part = lax.all_gather(key_rows, "seq", axis=0, tiled=True)
    value_rows_part = lax.all_gather(value_rows, "seq", axis=0, tiled=True)
    total_amount = key_rows_part.shape[0]
    scores, allowed, key_three_axes = scores_for(key_rows_part)
    masked = jnp.where(allowed, scores, masked_fill_value)
    new_top = jnp.maximum(row_top, jnp.max(masked, axis=-1))
    expo = jnp.where(allowed, jnp.exp(masked - new_top[..., None]), 0.0)
    row_sum = jnp.sum(expo, axis=-1)
    value_three_axes = value_rows_part.reshape(total_amount, KEY_VALUE_HEADS, HEAD_SIZE)
    summed = jnp.einsum(
        "hgqk,khd->hgqd",
        expo.astype(jnp.bfloat16),
        value_three_axes,
        preferred_element_type=jnp.float32,
    )
    row_top, row_sum, summed = (new_top, row_sum, summed)
    attended = summed / row_sum[..., None]
    log_total = row_top + jnp.log(row_sum)
    attended_b = (
        attended.transpose(2, 0, 1, 3)
        .reshape(token_rows, QUERY_HEADS * HEAD_SIZE)
        .astype(jnp.bfloat16)
    )
    middle = inputs + matmul(attended_b, out_all)
    norm2_all, gate_all, up_all, down_all = (
        lax.all_gather(norm2_gain, ("dp", "seq", "fsdp"), axis=0, tiled=True),
        lax.all_gather(w_gate, ("dp", "seq", "fsdp"), axis=0, tiled=True),
        lax.all_gather(w_up, ("dp", "seq", "fsdp"), axis=0, tiled=True),
        lax.all_gather(w_down, ("dp", "seq", "fsdp"), axis=0, tiled=True),
    )
    gain_two = norm2_all.astype(jnp.float32)
    normed2 = rms_scale(middle, gain_two).astype(jnp.bfloat16)
    gate_pre = matmul(normed2, gate_all)
    up_pre = matmul(normed2, up_all)
    hidden = (jax.nn.silu(gate_pre) * up_pre).astype(jnp.bfloat16)
    block_out = (middle + matmul(hidden, down_all)).astype(jnp.bfloat16)
    norm2_all, gate_all, up_all, down_all = (
        lax.all_gather(norm2_gain, ("dp", "seq", "fsdp"), axis=0, tiled=True),
        lax.all_gather(w_gate, ("dp", "seq", "fsdp"), axis=0, tiled=True),
        lax.all_gather(w_up, ("dp", "seq", "fsdp"), axis=0, tiled=True),
        lax.all_gather(w_down, ("dp", "seq", "fsdp"), axis=0, tiled=True),
    )
    all_parts = lax.axis_size(("dp", "seq", "fsdp"))
    grad_rows = out_grad[0]
    grad_float = grad_rows.astype(jnp.float32)
    down_sum = lax.psum_scatter(
        column_term(hidden, grad_rows), ("dp", "seq", "fsdp"), scatter_dimension=0, tiled=True
    )
    d_hidden = contract_cols(grad_rows, down_all)

    def swiglu(gate_in, up_in):
        return jax.nn.silu(gate_in) * up_in

    swiglu_out, swiglu_pull = jax.vjp(swiglu, gate_pre, up_pre)
    d_gate, d_up = swiglu_pull(d_hidden)
    d_gate_b = d_gate.astype(jnp.bfloat16)
    d_up_b = d_up.astype(jnp.bfloat16)
    gate_up_grads = jnp.concatenate([d_gate_b, d_up_b], axis=1)
    gate_up_sum = lax.psum_scatter(
        column_term(normed2, gate_up_grads), ("dp", "seq", "fsdp"), scatter_dimension=0, tiled=True
    )
    d_normed2 = contract_cols(d_gate_b, gate_all) + contract_cols(d_up_b, up_all)
    norm2_out, norm2_pull = jax.vjp(rms_scale, middle, gain_two)
    d_middle_norm, d_gain_two = norm2_pull(d_normed2)
    d_middle = grad_float + d_middle_norm
    norm1_all, query_all, key_all, value_all, out_all = (
        lax.all_gather(norm1_gain, ("dp", "seq", "fsdp"), axis=0, tiled=True),
        lax.all_gather(w_query, ("dp", "seq", "fsdp"), axis=0, tiled=True),
        lax.all_gather(key_weight, ("dp", "seq", "fsdp"), axis=0, tiled=True),
        lax.all_gather(value_weight, ("dp", "seq", "fsdp"), axis=0, tiled=True),
        lax.all_gather(w_out, ("dp", "seq", "fsdp"), axis=0, tiled=True),
    )
    d_branch = d_middle.astype(jnp.bfloat16)
    out_sum = lax.psum_scatter(
        column_term(attended_b, d_branch), ("dp", "seq", "fsdp"), scatter_dimension=0, tiled=True
    )
    attended_gradient = contract_cols(d_branch, out_all).astype(jnp.bfloat16)
    attended_grad_four = attended_gradient.reshape(
        token_rows, KEY_VALUE_HEADS, queries_per_group, HEAD_SIZE
    ).transpose(1, 2, 0, 3)
    delta_rows = jnp.sum(attended_grad_four.astype(jnp.float32) * attended, axis=-1)
    key_rows_part = lax.all_gather(key_rows, "seq", axis=0, tiled=True)
    value_rows_part = lax.all_gather(value_rows, "seq", axis=0, tiled=True)
    total_amount = key_rows_part.shape[0]
    scores, allowed, key_three_axes = scores_for(key_rows_part)
    probs = jnp.where(allowed, jnp.exp(scores - log_total[..., None]), 0.0)
    value_three_axes = value_rows_part.reshape(total_amount, KEY_VALUE_HEADS, HEAD_SIZE)
    value_gradient = jnp.einsum(
        "hgqk,hgqd->khd",
        probs.astype(jnp.bfloat16),
        attended_grad_four,
        preferred_element_type=jnp.float32,
    )
    d_probs = jnp.einsum(
        "hgqd,khd->hgqk", attended_grad_four, value_three_axes, preferred_element_type=jnp.float32
    )
    d_scores = (probs * (d_probs - delta_rows[..., None])).astype(jnp.bfloat16)
    d_query_acc = (
        jnp.einsum("hgqk,khd->hgqd", d_scores, key_three_axes, preferred_element_type=jnp.float32)
        * score_scale
    )
    local_key_gradient = (
        jnp.einsum("hgqk,qhgd->khd", d_scores, query_four_axes, preferred_element_type=jnp.float32)
        * score_scale
    )
    every_key_gradient = local_key_gradient.reshape(total_amount, KEY_VALUE_HEADS * HEAD_SIZE)
    every_value_gradient = value_gradient.reshape(total_amount, KEY_VALUE_HEADS * HEAD_SIZE)
    d_query_acc, every_key_gradient, every_value_gradient = (
        d_query_acc,
        every_key_gradient,
        every_value_gradient,
    )
    d_keys_own, d_values_own = (
        lax.psum_scatter(
            every_key_gradient.astype(jnp.bfloat16), "seq", scatter_dimension=0, tiled=True
        ).astype(jnp.float32),
        lax.psum_scatter(
            every_value_gradient.astype(jnp.bfloat16), "seq", scatter_dimension=0, tiled=True
        ).astype(jnp.float32),
    )
    d_query_rows = rounded(
        d_query_acc.transpose(2, 0, 1, 3).reshape(token_rows, QUERY_HEADS * HEAD_SIZE)
    )
    query_out, query_pull = jax.vjp(query_part, query_raw, gain_query)
    d_query_raw, d_gain_query = query_pull(d_query_rows)
    key_out, key_pull = jax.vjp(key_part, key_unnormed, gain_key)
    d_key_raw, d_gain_key = key_pull(rounded(d_keys_own))
    d_query_b = d_query_raw.astype(jnp.bfloat16)
    d_key_b = d_key_raw.astype(jnp.bfloat16)
    d_value_b = d_values_own.astype(jnp.bfloat16)
    projection_grads = jnp.concatenate([d_query_b, d_key_b, d_value_b], axis=1)
    projection_sum = lax.psum_scatter(
        column_term(normed1, projection_grads),
        ("dp", "seq", "fsdp"),
        scatter_dimension=0,
        tiled=True,
    )
    d_normed1 = (
        contract_cols(d_query_b, query_all)
        + contract_cols(d_key_b, key_all)
        + contract_cols(d_value_b, value_all)
    )
    norm1_out, norm1_pull = jax.vjp(rms_scale, inputs, gain_one)
    d_input_norm, d_gain_one = norm1_pull(d_normed1)
    gain_sums = lax.psum((d_gain_one, d_gain_two, d_gain_query, d_gain_key), ("dp", "seq", "fsdp"))
    input_grad = (d_middle + d_input_norm).astype(jnp.bfloat16)
    width_share = MODEL_WIDTH // all_parts
    share_start = lax.axis_index(("dp", "seq", "fsdp")) * width_share
    gain_one_own = lax.dynamic_slice_in_dim(gain_sums[0], share_start, width_share)
    gain_two_own = lax.dynamic_slice_in_dim(gain_sums[1], share_start, width_share)
    query_cols = QUERY_HEADS * HEAD_SIZE
    kv_cols = KEY_VALUE_HEADS * HEAD_SIZE
    grad_query = projection_sum[:, :query_cols]
    grad_key = projection_sum[:, query_cols : query_cols + kv_cols]
    grad_value = projection_sum[:, query_cols + kv_cols :]
    grad_gate = gate_up_sum[:, :FF]
    grad_up = gate_up_sum[:, FF:]
    return (
        block_out[None],
        input_grad[None],
        gain_one_own,
        grad_query,
        grad_key,
        grad_value,
        out_sum,
        gain_sums[2],
        gain_sums[3],
        gain_two_own,
        grad_gate,
        grad_up,
        down_sum,
    )


def solution(mesh):
    in_specs = (
        P(("dp", "fsdp"), "seq", None),
        P(("dp", "fsdp"), "seq", None),
        P(("dp", "fsdp"), None),
        P(("dp", "fsdp"), "seq"),
        P(("dp", "seq", "fsdp")),
        P(("dp", "seq", "fsdp"), None),
        P(("dp", "seq", "fsdp"), None),
        P(("dp", "seq", "fsdp"), None),
        P(("dp", "seq", "fsdp"), None),
        P(),
        P(),
        P(("dp", "seq", "fsdp")),
        P(("dp", "seq", "fsdp"), None),
        P(("dp", "seq", "fsdp"), None),
        P(("dp", "seq", "fsdp"), None),
    )
    out_specs = (
        P(("dp", "fsdp"), "seq", None),
        P(("dp", "fsdp"), "seq", None),
        P(("dp", "seq", "fsdp")),
        P(("dp", "seq", "fsdp"), None),
        P(("dp", "seq", "fsdp"), None),
        P(("dp", "seq", "fsdp"), None),
        P(("dp", "seq", "fsdp"), None),
        P(),
        P(),
        P(("dp", "seq", "fsdp")),
        P(("dp", "seq", "fsdp"), None),
        P(("dp", "seq", "fsdp"), None),
        P(("dp", "seq", "fsdp"), None),
    )
    return jax.shard_map(body, mesh=mesh, in_specs=in_specs, out_specs=out_specs, check_vma=False)
```

profile of v0, /device:TPU:0, one launch (start us, length us, event | category | flops | bytes accessed | tf_op | source)
XLA Modules:
  0.0 1537.1 jit_solution(15862183328871471143)
XLA Ops:
  10.4 42.0 %all-reduce.7 = (bf16[1024]{0:T(1024)(128)(2,1)S(1)}, bf16[1024]{0:T(1024)(128)(2,1)S(1)}) all-reduce(bf16[1024]{0:T(1024)(128)(2,1)S(1)} %dynamic-update-slice, bf16[1024]{0:T(1024)(128)(2,1)S(1)} %dynamic-update-slice.1), channel_id=1, replica_groups=mesh['dp'=2,'seq'=4,'fsdp'=4] {'dp','seq','fsdp'}, use_global_device_ids=true, to_apply=%add.4 | all-reduce | flops 2048 | bytes 8192
  53.7 13.8 all-gather.16.cloned.1.call-done
  67.5 2.6 convolution_convert_fusion.1
  72.3 50.9 %all-gather.10.cloned.1.call-done = bf16[1024,512]{1,0:T(8,128)(2,1)} async-done(((bf16[32,512]{1,0:T(8,128)(2,1)}), bf16[1024,512]{1,0:T(8,128)(2,1)}) %all-gather.10.cloned.1.call-update) | async-done | bytes 1048592 | tf_op jit(solution)/shard_map/all_gather | solution.py:106
  124.8 1.6 multiply_reduce_fusion.9
  132.3 8.8 all-gather.18.cloned.1.call-done
  142.6 57.8 %all-gather.14.cloned.1.call-done = bf16[1024,1024]{1,0:T(8,128)(2,1)} async-done(((bf16[32,1024]{1,0:T(8,128)(2,1)}), bf16[1024,1024]{1,0:T(8,128)(2,1)}) %all-gather.14.cloned.1.call-update) | async-done | bytes 2097168 | tf_op jit(solution)/shard_map/all_gather | solution.py:105
  200.5 3.9 copy.48
  204.4 2.4 multiply_reduce_fusion.6
  208.4 9.8 all-gather.12.cloned.1.call-done
  218.2 3.7 fusion.2
  221.9 4.0 fusion.4
  226.0 1.6 copy-done
  228.0 4.7 fusion.52
  232.7 44.7 %all-gather.20.cloned.1.call-done = bf16[1024,1024]{1,0:T(8,128)(2,1)} async-done(((bf16[32,1024]{1,0:T(8,128)(2,1)}), bf16[1024,1024]{1,0:T(8,128)(2,1)}) %all-gather.20.cloned.1.call-update) | async-done | bytes 2097168 | tf_op jit(solution)/shard_map/all_gather | solution.py:108
  277.5 2.6 multiply_reduce_fusion.5
  282.0 1.6 multiply_convert_fusion.3
  283.7 77.6 %all-gather.24.cloned.1.call-done = bf16[1024,4608]{1,0:T(8,128)(2,1)} async-done(((bf16[32,4608]{1,0:T(8,128)(2,1)}), bf16[1024,4608]{1,0:T(8,128)(2,1)}) %all-gather.24.cloned.1.call-update) | async-done | bytes 9437200 | tf_op jit(solution)/shard_map/all_gather | solution.py:179
  361.3 8.6 fusion.90
  369.9 75.0 %all-gather.22.cloned.1.call-done = bf16[1024,4608]{1,0:T(8,128)(2,1)} async-done(((bf16[32,4608]{1,0:T(8,128)(2,1)}), bf16[1024,4608]{1,0:T(8,128)(2,1)}) %all-gather.22.cloned.1.call-update) | async-done | bytes 9437200 | tf_op jit(solution)/shard_map/all_gather | solution.py:178
  444.9 8.6 fusion.89
  453.5 75.0 %all-gather.26.cloned.1.call-done = bf16[4608,1024]{1,0:T(8,128)(2,1)} async-done(((bf16[144,1024]{1,0:T(8,128)(2,1)}), bf16[4608,1024]{1,0:T(8,128)(2,1)}) %all-gather.26.cloned.1.call-update) | async-done | bytes 9437200 | tf_op jit(solution)/shard_map/all_gather | solution.py:180
  528.5 10.5 multiply_convert_fusion.1
  539.0 2.6 fusion.91
  541.7 6.2 multiply_reduce_fusion
  549.5 1.6 convolution_convert_fusion
  551.1 2.0 copy.51
  553.1 1.6 multiply_reduce_fusion.3
  554.7 11.6 multiply_convert_fusion
  566.3 3.6 fusion.20
  570.4 5.3 fusion.28
  576.7 10.2 bitcast_convert_fusion
  588.2 1.8 multiply_reduce_fusion.1
  590.7 1.9 fusion.41
  597.5 23.6 %reduce-scatter.9.cloned.1.call-done = bf16[256,512]{0,1:T(8,128)(2,1)} async-done(((bf16[1024,512]{0,1:T(8,128)(2,1)}), bf16[256,512]{0,1:T(8,128)(2,1)}) %reduce-scatter.9.cloned.1.call-update) | async-done | bytes 262160 | tf_op jit(solution)/shard_map/reduce_scatter | solution.py:268
  621.2 5.9 fusion.46
  627.2 17.3 %fusion.15 = f32[1024,9216]{1,0:T(8,128)} fusion(bf16[256,1024]{1,0:T(8,128)(2,1)S(1)} %copy-done.6, bf16[256,4608]{1,0:T(8,128)(2,1)} %copy-done.11, bf16[256,4608]{1,0:T(8,128)(2,1)} %copy-done.12), kind=kOutput, calls=%fused_computation.18 | convolution fusion | flops 4841275392 | bytes 42991616 | tf_op jit(solution)/shard_map/dot_general | solution.py:61
  645.5 2.7 fusion.65
  648.4 9.7 fusion.61
  659.1 2.4 fusion.92
  661.5 8.0 fusion.31
  670.8 42.7 %all-reduce.6 = (f32[1024]{0:T(1024)S(1)}, f32[64]{0:T(128)}, f32[64]{0:T(128)}, f32[1024]{0:T(1024)S(1)}) all-reduce(f32[1024]{0:T(1024)S(1)} %get-tuple-element.17, f32[64]{0:T(128)S(1)} %copy-done.41, f32[64]{0:T(128)S(1)} %get-tuple-element.19, f32[1024]{0:T(1024)S(1)} %copy-done.40), channel_id=1, replica_groups=mesh['dp'=2,'seq'=4,'fsdp'=4] {'dp','seq','fsdp'}, use_global_device_ids=true, to_apply=%region_16.17 | all-reduce | flops 2176 | bytes 17408 | tf_op jit(solution)/shard_map/psum | solution.py:296
  715.8 98.3 %reduce-scatter.11.cloned.1.call-done = f32[32,2048]{1,0:T(8,128)} async-done(((f32[1024,2048]{1,0:T(8,128)}), f32[32,2048]{1,0:T(8,128)}) %reduce-scatter.11.cloned.1.call-update) | async-done | bytes 262160 | tf_op jit(solution)/shard_map/reduce_scatter | solution.py:283
  814.1 1.6 slice.40
  817.2 349.6 %reduce-scatter.15.cloned.1.call-done = f32[32,9216]{1,0:T(8,128)} async-done(((f32[1024,9216]{1,0:T(8,128)}), f32[32,9216]{1,0:T(8,128)}) %reduce-scatter.15.cloned.1.call-update) | async-done | bytes 1179664 | tf_op jit(solution)/shard_map/reduce_scatter | solution.py:210
  1166.9 2.3 fusion.87
  1169.2 147.9 %reduce-scatter.13.cloned.1.call-done = f32[32,1024]{1,0:T(8,128)} async-done(((f32[1024,1024]{1,0:T(8,128)}), f32[32,1024]{1,0:T(8,128)}) %reduce-scatter.13.cloned.1.call-update) | async-done | bytes 131088 | tf_op jit(solution)/shard_map/reduce_scatter | solution.py:225
  1317.1 213.3 %reduce-scatter.17.cloned.1.call-done = f32[144,1024]{1,0:T(8,128)} async-done(((f32[4608,1024]{1,0:T(8,128)}), f32[144,1024]{1,0:T(8,128)}) %reduce-scatter.17.cloned.1.call-update) | async-done | bytes 589840 | tf_op jit(solution)/shard_map/reduce_scatter | solution.py:197
  (167 shorter events, 36.7 us)
Async XLA Ops:
  7.2 123.9 %copy-start.42 = (bf16[64]{0:T(256)(128)(2,1)S(1)}, bf16[64]{0:T(256)(128)(2,1)}, u32[]{:S(2)}) copy-start(bf16[64]{0:T(256)(128)(2,1)} %param.24) | copy-start | bytes 388
  7.2 123.9 %copy-start.43 = (s32[1,4]{1,0:T(1,128)S(1)}, s32[1,4]{1,0:T(1,128)}, u32[]{:S(2)}) copy-start(s32[1,4]{1,0:T(1,128)} %param.17) | copy-start | bytes 52
  7.2 60.3 %all-gather.16.cloned.1.call-start = ((), (), s32[]{:S(2)}) async-start(), calls=%async_computation.9 | async-start | bytes 1081344 | tf_op jit(solution)/shard_map/all_gather | solution.py:107
  7.9 115.3 %all-gather.10.cloned.1.call-start = ((), (), s32[]{:S(2)}) async-start(), calls=%async_computation.6 | async-start | bytes 1081344 | tf_op jit(solution)/shard_map/all_gather | solution.py:106
  8.7 132.4 %all-gather.18.cloned.1.call-start = ((), (), s32[]{:S(2)}) async-start(), calls=%async_computation.10 | async-start | bytes 1310720 | tf_op jit(solution)/shard_map/all_gather | solution.py:153
  52.5 151.9 %copy-start.21 = (f32[1024]{0:T(1024)}, f32[1024]{0:T(1024)S(1)}, u32[]{:S(2)}) copy-start(f32[1024]{0:T(1024)S(1)} %convert_element_type.154) | copy-start | bytes 12292
  53.7 18.4 %copy-start.31 = (f32[256]{0:T(256)}, f32[256]{0:T(256)S(1)}, u32[]{:S(2)}) copy-start(f32[256]{0:T(256)S(1)} %fusion.34) | copy-start | bytes 3076
  53.7 150.7 %copy-start.29 = (f32[256]{0:T(256)}, f32[256]{0:T(256)S(1)}, u32[]{:S(2)}) copy-start(f32[256]{0:T(256)S(1)} %fusion.78) | copy-start | bytes 3076
  70.1 134.3 %copy-start.2 = (bf16[1,256,1024]{2,1,0:T(8,128)(2,1)S(1)}, bf16[1,256,1024]{2,1,0:T(8,128)(2,1)}, u32[]{:S(2)}) copy-start(bf16[1,256,1024]{2,1,0:T(8,128)(2,1)} %param.15) | copy-start | bytes 1572868
  70.1 130.3 %all-gather.14.cloned.1.call-start = ((), (), s32[]{:S(2)}) async-start(), calls=%async_computation.8 | async-start | bytes 2162688 | tf_op jit(solution)/shard_map/all_gather | solution.py:105
  70.7 147.4 %all-gather.12.cloned.1.call-start = ((), (), s32[]{:S(2)}) async-start(), calls=%async_computation.7 | async-start | bytes 1310720 | tf_op jit(solution)/shard_map/all_gather | solution.py:152
  71.4 135.4 %copy-start.37 = (f32[64]{0:T(128)}, f32[64]{0:T(128)S(1)}, u32[]{:S(2)}) copy-start(f32[64]{0:T(128)S(1)} %convert_element_type.157) | copy-start | bytes 772
  128.1 149.4 %all-gather.20.cloned.1.call-start = ((), (), s32[]{:S(2)}) async-start(), calls=%async_computation.11 | async-start | bytes 2162688 | tf_op jit(solution)/shard_map/all_gather | solution.py:108
  128.6 232.7 %all-gather.24.cloned.1.call-start = ((), (), s32[]{:S(2)}) async-start(), calls=%async_computation.13 | async-start | bytes 9732096 | tf_op jit(solution)/shard_map/all_gather | solution.py:179
  129.4 315.5 %all-gather.22.cloned.1.call-start = ((), (), s32[]{:S(2)}) async-start(), calls=%async_computation.12 | async-start | bytes 9732096 | tf_op jit(solution)/shard_map/all_gather | solution.py:178
  130.1 398.3 %all-gather.26.cloned.1.call-start = ((), (), s32[]{:S(2)}) async-start(), calls=%async_computation.14 | async-start | bytes 9732096 | tf_op jit(solution)/shard_map/all_gather | solution.py:180
  130.9 462.7 %reduce-scatter.7.cloned.1.call-start = ((), (), s32[]{:S(2)}) async-start(), calls=%async_computation.15 | async-start | bytes 1310720 | tf_op jit(solution)/shard_map/reduce_scatter | solution.py:265
  131.1 76.1 %copy-start.39 = (f32[64]{0:T(128)}, f32[64]{0:T(128)S(1)}, u32[]{:S(2)}) copy-start(f32[64]{0:T(128)S(1)} %convert_element_type.162) | copy-start | bytes 772
  142.6 83.4 %copy-start.18 = (bf16[1024,512]{0,1:T(8,128)(2,1)}, bf16[1024,512]{0,1:T(8,128)(2,1)S(1)}, u32[]{:S(2)}) copy-start(bf16[1024,512]{0,1:T(8,128)(2,1)S(1)} %copy.49) | copy-start | bytes 3145732
  221.9 4.1 copy-start.23
  221.9 5.7 copy-start
  280.1 261.5 %copy-start.4 = (f32[256,1024]{1,0:T(8,128)}, f32[256,1024]{1,0:T(8,128)S(1)}, u32[]{:S(2)}) copy-start(f32[256,1024]{1,0:T(8,128)S(1)} %get-tuple-element.53) | copy-start | bytes 3145732
  528.5 10.5 copy-start.3
  539.0 2.7 copy-start.26
  539.0 2.7 copy-start.36
  541.7 6.3 copy-start.34
  541.7 6.3 copy-start.13
  541.7 7.8 copy-start.7
  566.3 3.6 copy-start.1
  569.9 51.3 %reduce-scatter.9.cloned.1.call-start = ((), (), s32[]{:S(2)}) async-start(), calls=%async_computation.16 | async-start | bytes 1310720 | tf_op jit(solution)/shard_map/reduce_scatter | solution.py:268
  586.9 7.8 copy-start.20
  586.9 7.8 copy-start.38
  586.9 9.3 copy-start.28
  586.9 227.2 %reduce-scatter.11.cloned.1.call-start = ((), (), s32[]{:S(2)}) async-start(), calls=%async_computation.17 | async-start | bytes 8650752 | tf_op jit(solution)/shard_map/reduce_scatter | solution.py:283
  621.2 6.0 copy-start.6
  627.1 539.8 %reduce-scatter.15.cloned.1.call-start = ((), (), s32[]{:S(2)}) async-start(), calls=%async_computation.19 | async-start | bytes 38928384 | tf_op jit(solution)/shard_map/reduce_scatter | solution.py:210
  644.4 3.9 copy-start.14
  644.4 672.7 %reduce-scatter.13.cloned.1.call-start = ((), (), s32[]{:S(2)}) async-start(), calls=%async_computation.18 | async-start | bytes 4325376 | tf_op jit(solution)/shard_map/reduce_scatter | solution.py:225
  648.2 882.2 %reduce-scatter.17.cloned.1.call-start = ((), (), s32[]{:S(2)}) async-start(), calls=%async_computation.20 | async-start | bytes 19464192 | tf_op jit(solution)/shard_map/reduce_scatter | solution.py:197
  658.0 3.4 copy-start.5
  661.5 8.1 copy-start.10
  661.5 8.6 copy-start.16
  661.5 8.6 copy-start.17
  661.5 8.6 copy-start.22
  661.5 8.6 copy-start.30
  661.5 9.3 copy-start.40
  661.5 9.3 copy-start.41
  661.5 53.2 %copy-start.32 = (f32[256]{0:T(256)S(1)}, f32[256]{0:T(256)}, u32[]{:S(2)}) copy-start(f32[256]{0:T(256)} %copy-done.31) | copy-start | bytes 3076
  (11 other events, 15.1 us)
Sparse Core Ops, SparseCore 0:
  11.0 56.4 all-gather.15
  70.5 52.7 all-gather.9
  125.4 15.6 all-gather.17
  143.9 56.4 all-gather.13
  202.4 15.6 all-gather.11
  221.0 56.4 all-gather.19
  280.4 80.8 all-gather.23
  364.2 80.6 all-gather.21
  447.8 80.6 all-gather.25
  570.0 23.5 reduce-scatter.6
  596.3 24.8 reduce-scatter.8
  627.2 186.8 reduce-scatter.10
  820.6 346.2 reduce-scatter.14
  1169.7 147.4 reduce-scatter.12
  1325.1 205.2 reduce-scatter.16
where the time goes:
time: 1540 us
  waiting for transfers between devices  1250 us (81%)
  matrix products  133 us (9%)
  blocking collectives  84.8 us (6%)
  other arithmetic  28.1 us (2%)
  local copies, waits for them, and re-layouts  22.9 us (1%)
    reduce_scatter x1, waiting for transfers between devices, body(): lax.psum_scatter(column_term(normed2, gate_up_grads), ('dp', 'seq', 'fsdp...  350 us
    reduce_scatter x1, waiting for transfers between devices, body(): lax.psum_scatter(column_term(hidden, grad_rows), ('dp', 'seq', 'fsdp'), s...  213 us
    reduce_scatter x1, waiting for transfers between devices, body(): lax.psum_scatter(column_term(attended_b, d_branch), ('dp', 'seq', 'fsdp')...  148 us
    reduce_scatter x1, waiting for transfers between devices, body(): lax.psum_scatter(column_term(normed1, projection_grads), ('dp', 'seq', 'f...  98.3 us
    all_gather x1, waiting for transfers between devices, body(): lax.all_gather(w_up, ('dp', 'seq', 'fsdp'), axis=0, tiled=True)  77.6 us
    all_gather x1, waiting for transfers between devices, body(): lax.all_gather(w_gate, ('dp', 'seq', 'fsdp'), axis=0, tiled=True)  75 us
    all_gather x1, waiting for transfers between devices, body(): lax.all_gather(w_down, ('dp', 'seq', 'fsdp'), axis=0, tiled=True)  75 us
    all_gather x1, waiting for transfers between devices, body(): lax.all_gather(w_query, ('dp', 'seq', 'fsdp'), axis=0, tiled=True)  57.8 us
  transfers between devices with their start and end apart: 15, of which 15 were waited for; matrix products, arithmetic and copies ran while one was open for 9% of the time, Pallas kernels for 0%

commit v1 on v0

--- a/solution.py
+++ b/solution.py
@@ -100,19 +100,56 @@
     own_segments = lax.dynamic_slice_in_dim(segments, own_offset, token_rows)
     own_places = own_offset + jnp.arange(token_rows, dtype=jnp.int32)
     cosine_table, sine_table = rotary_tables(positions[0])
-    norm1_all, query_all, key_all, value_all, out_all = (
-        lax.all_gather(norm1_gain, ("dp", "seq", "fsdp"), axis=0, tiled=True),
-        lax.all_gather(w_query, ("dp", "seq", "fsdp"), axis=0, tiled=True),
-        lax.all_gather(key_weight, ("dp", "seq", "fsdp"), axis=0, tiled=True),
-        lax.all_gather(value_weight, ("dp", "seq", "fsdp"), axis=0, tiled=True),
-        lax.all_gather(w_out, ("dp", "seq", "fsdp"), axis=0, tiled=True),
-    )
+    weight_rows = w_query.shape[0]
+    query_cols = QUERY_HEADS * HEAD_SIZE
+    kv_cols = KEY_VALUE_HEADS * HEAD_SIZE
+    qkv_cols = query_cols + 2 * kv_cols
+    packed = jnp.concatenate(
+        [
+            w_query,
+            key_weight,
+            value_weight,
+            w_out,
+            norm1_gain[:, None],
+            norm2_gain[:, None],
+            jnp.zeros((weight_rows, 126), jnp.bfloat16),
+        ],
+        axis=1,
+    )
+    packed = lax.all_gather(packed, ("dp", "seq", "fsdp"), axis=0, tiled=True)
+    qkv_all = packed[:, :qkv_cols]
+    out_all = packed[:, qkv_cols : qkv_cols + MODEL_WIDTH]
+    norm1_all = packed[:, qkv_cols + MODEL_WIDTH]
+    norm2_all = packed[:, qkv_cols + MODEL_WIDTH + 1]
+
+    dp_parts = lax.axis_size("dp")
+    fsdp_parts = lax.axis_size("fsdp")
+    unit_rows = w_down.shape[0]
+    units = dp_parts * fsdp_parts * unit_rows
+
+    def by_owner(columns):
+        split = columns.reshape(weight_rows, dp_parts, seq_parts, fsdp_parts, unit_rows)
+        return split.transpose(2, 0, 1, 3, 4).reshape(seq_parts, weight_rows, units)
+
+    gate_up = jnp.concatenate([by_owner(w_gate), by_owner(w_up)], axis=2)
+    gate_up = lax.all_to_all(gate_up, "seq", 0, 0)
+    gate_up = lax.all_gather(
+        gate_up.reshape(seq_parts * weight_rows, 2 * units), ("dp", "fsdp"), axis=0, tiled=True
+    )
+    gate_up = (
+        gate_up.reshape(dp_parts, fsdp_parts, seq_parts, weight_rows, 2 * units)
+        .transpose(0, 2, 1, 3, 4)
+        .reshape(MODEL_WIDTH, 2 * units)
+    )
+    down_all = lax.all_gather(w_down, ("dp", "fsdp"), axis=0, tiled=True)
+    grad_all = lax.all_gather(out_grad[0], "seq", axis=0, tiled=True)
     inputs = tokens[0].astype(jnp.float32)
     gain_one = norm1_all.astype(jnp.float32)
     normed1 = rms_scale(inputs, gain_one).astype(jnp.bfloat16)
-    query_raw = matmul(normed1, query_all)
-    key_unnormed = matmul(normed1, key_all)
-    value_raw = matmul(normed1, value_all)
+    qkv_raw = matmul(normed1, qkv_all)
+    query_raw = qkv_raw[:, :query_cols]
+    key_unnormed = qkv_raw[:, query_cols : query_cols + kv_cols]
+    value_raw = qkv_raw[:, query_cols + kv_cols :]
     gain_query = q_gain.astype(jnp.float32)
     gain_key = k_gain.astype(jnp.float32)
 
@@ -149,8 +186,11 @@
         (KEY_VALUE_HEADS, queries_per_group, token_rows), masked_fill_value, jnp.float32
     )
     row_top = starting_maximum
-    key_rows_part = lax.all_gather(key_rows, "seq", axis=0, tiled=True)
-    value_rows_part = lax.all_gather(value_rows, "seq", axis=0, tiled=True)
+    both_rows = lax.all_gather(
+        jnp.concatenate([key_rows, value_rows], axis=1), "seq", axis=0, tiled=True
+    )
+    key_rows_part = both_rows[:, :kv_cols]
+    value_rows_part = both_rows[:, kv_cols:]
     total_amount = key_rows_part.shape[0]
     scores, allowed, key_three_axes = scores_for(key_rows_part)
     masked = jnp.where(allowed, scores, masked_fill_value)
@@ -173,66 +213,69 @@
         .astype(jnp.bfloat16)
     )
     middle = inputs + matmul(attended_b, out_all)
-    norm2_all, gate_all, up_all, down_all = (
-        lax.all_gather(norm2_gain, ("dp", "seq", "fsdp"), axis=0, tiled=True),
-        lax.all_gather(w_gate, ("dp", "seq", "fsdp"), axis=0, tiled=True),
-        lax.all_gather(w_up, ("dp", "seq", "fsdp"), axis=0, tiled=True),
-        lax.all_gather(w_down, ("dp", "seq", "fsdp"), axis=0, tiled=True),
-    )
     gain_two = norm2_all.astype(jnp.float32)
     normed2 = rms_scale(middle, gain_two).astype(jnp.bfloat16)
-    gate_pre = matmul(normed2, gate_all)
-    up_pre = matmul(normed2, up_all)
-    hidden = (jax.nn.silu(gate_pre) * up_pre).astype(jnp.bfloat16)
-    block_out = (middle + matmul(hidden, down_all)).astype(jnp.bfloat16)
-    norm2_all, gate_all, up_all, down_all = (
-        lax.all_gather(norm2_gain, ("dp", "seq", "fsdp"), axis=0, tiled=True),
-        lax.all_gather(w_gate, ("dp", "seq", "fsdp"), axis=0, tiled=True),
-        lax.all_gather(w_up, ("dp", "seq", "fsdp"), axis=0, tiled=True),
-        lax.all_gather(w_down, ("dp", "seq", "fsdp"), axis=0, tiled=True),
-    )
-    all_parts = lax.axis_size(("dp", "seq", "fsdp"))
+    normed2_all = lax.all_gather(normed2, "seq", axis=0, tiled=True)
+    gate_up_pre = matmul(normed2_all, gate_up)
+    gate_pre = gate_up_pre[:, :units]
+    up_pre = gate_up_pre[:, units:]
+
+    def swiglu(gate_in, up_in):
+        return jax.nn.silu(gate_in) * up_in
+
+    swiglu_out, swiglu_pull = jax.vjp(swiglu, gate_pre, up_pre)
+    hidden = swiglu_out.astype(jnp.bfloat16)
+    d_hidden = contract_cols(grad_all, down_all)
+    d_gate, d_up = swiglu_pull(d_hidden)
+    gate_up_grads = jnp.concatenate([d_gate.astype(jnp.bfloat16), d_up.astype(jnp.bfloat16)], axis=1)
+    d_normed2 = contract_cols(gate_up_grads, gate_up).astype(jnp.bfloat16)
+    d_normed2 = lax.psum_scatter(d_normed2, "seq", scatter_dimension=0, tiled=True)
+    d_normed2 = d_normed2.astype(jnp.float32)
+    branch = lax.psum_scatter(
+        matmul(hidden, down_all).astype(jnp.bfloat16), "seq", scatter_dimension=0, tiled=True
+    )
+    block_out = (middle + branch.astype(jnp.float32)).astype(jnp.bfloat16)
+    down_sum = lax.psum_scatter(
+        column_term(hidden, grad_all).astype(jnp.bfloat16),
+        ("dp", "fsdp"),
+        scatter_dimension=0,
+        tiled=True,
+    ).astype(jnp.float32)
+    gate_up_sum = (
+        column_term(normed2_all, gate_up_grads)
+        .astype(jnp.bfloat16)
+        .reshape(dp_parts, seq_parts, fsdp_parts, weight_rows, 2 * units)
+        .transpose(0, 2, 1, 3, 4)
+        .reshape(MODEL_WIDTH, 2 * units)
+    )
+    gate_up_sum = lax.psum_scatter(gate_up_sum, ("dp", "fsdp"), scatter_dimension=0, tiled=True)
+    gate_up_sum = lax.all_to_all(
+        gate_up_sum.reshape(seq_parts, weight_rows, 2 * units), "seq", 0, 0
+    )
+
+    def to_columns(owned):
+        split = owned.reshape(seq_parts, weight_rows, dp_parts, fsdp_parts, unit_rows)
+        return split.transpose(1, 2, 0, 3, 4).reshape(weight_rows, FF).astype(jnp.float32)
+
+    grad_gate = to_columns(gate_up_sum[:, :, :units])
+    grad_up = to_columns(gate_up_sum[:, :, units:])
     grad_rows = out_grad[0]
     grad_float = grad_rows.astype(jnp.float32)
-    down_sum = lax.psum_scatter(
-        column_term(hidden, grad_rows), ("dp", "seq", "fsdp"), scatter_dimension=0, tiled=True
-    )
-    d_hidden = contract_cols(grad_rows, down_all)
-
-    def swiglu(gate_in, up_in):
-        return jax.nn.silu(gate_in) * up_in
-
-    swiglu_out, swiglu_pull = jax.vjp(swiglu, gate_pre, up_pre)
-    d_gate, d_up = swiglu_pull(d_hidden)
-    d_gate_b = d_gate.astype(jnp.bfloat16)
-    d_up_b = d_up.astype(jnp.bfloat16)
-    gate_up_grads = jnp.concatenate([d_gate_b, d_up_b], axis=1)
-    gate_up_sum = lax.psum_scatter(
-        column_term(normed2, gate_up_grads), ("dp", "seq", "fsdp"), scatter_dimension=0, tiled=True
-    )
-    d_normed2 = contract_cols(d_gate_b, gate_all) + contract_cols(d_up_b, up_all)
     norm2_out, norm2_pull = jax.vjp(rms_scale, middle, gain_two)
     d_middle_norm, d_gain_two = norm2_pull(d_normed2)
     d_middle = grad_float + d_middle_norm
-    norm1_all, query_all, key_all, value_all, out_all = (
-        lax.all_gather(norm1_gain, ("dp", "seq", "fsdp"), axis=0, tiled=True),
-        lax.all_gather(w_query, ("dp", "seq", "fsdp"), axis=0, tiled=True),
-        lax.all_gather(key_weight, ("dp", "seq", "fsdp"), axis=0, tiled=True),
-        lax.all_gather(value_weight, ("dp", "seq", "fsdp"), axis=0, tiled=True),
-        lax.all_gather(w_out, ("dp", "seq", "fsdp"), axis=0, tiled=True),
-    )
     d_branch = d_middle.astype(jnp.bfloat16)
     out_sum = lax.psum_scatter(
-        column_term(attended_b, d_branch), ("dp", "seq", "fsdp"), scatter_dimension=0, tiled=True
-    )
+        column_term(attended_b, d_branch).astype(jnp.bfloat16),
+        ("dp", "seq", "fsdp"),
+        scatter_dimension=0,
+        tiled=True,
+    ).astype(jnp.float32)
     attended_gradient = contract_cols(d_branch, out_all).astype(jnp.bfloat16)
     attended_grad_four = attended_gradient.reshape(
         token_rows, KEY_VALUE_HEADS, queries_per_group, HEAD_SIZE
     ).transpose(1, 2, 0, 3)
     delta_rows = jnp.sum(attended_grad_four.astype(jnp.float32) * attended, axis=-1)
-    key_rows_part = lax.all_gather(key_rows, "seq", axis=0, tiled=True)
-    value_rows_part = lax.all_gather(value_rows, "seq", axis=0, tiled=True)
-    total_amount = key_rows_part.shape[0]
     scores, allowed, key_three_axes = scores_for(key_rows_part)
     probs = jnp.where(allowed, jnp.exp(scores - log_total[..., None]), 0.0)
     value_three_axes = value_rows_part.reshape(total_amount, KEY_VALUE_HEADS, HEAD_SIZE)
@@ -256,56 +299,42 @@
     )
     every_key_gradient = local_key_gradient.reshape(total_amount, KEY_VALUE_HEADS * HEAD_SIZE)
     every_value_gradient = value_gradient.reshape(total_amount, KEY_VALUE_HEADS * HEAD_SIZE)
-    d_query_acc, every_key_gradient, every_value_gradient = (
-        d_query_acc,
-        every_key_gradient,
-        every_value_gradient,
-    )
-    d_keys_own, d_values_own = (
-        lax.psum_scatter(
-            every_key_gradient.astype(jnp.bfloat16), "seq", scatter_dimension=0, tiled=True
-        ).astype(jnp.float32),
-        lax.psum_scatter(
-            every_value_gradient.astype(jnp.bfloat16), "seq", scatter_dimension=0, tiled=True
-        ).astype(jnp.float32),
-    )
+    d_both_own = lax.psum_scatter(
+        jnp.concatenate([every_key_gradient, every_value_gradient], axis=1).astype(jnp.bfloat16),
+        "seq",
+        scatter_dimension=0,
+        tiled=True,
+    )
+    d_keys_own = d_both_own[:, :kv_cols].astype(jnp.float32)
+    d_values_own = d_both_own[:, kv_cols:]
     d_query_rows = rounded(
         d_query_acc.transpose(2, 0, 1, 3).reshape(token_rows, QUERY_HEADS * HEAD_SIZE)
     )
     query_out, query_pull = jax.vjp(query_part, query_raw, gain_query)
     d_query_raw, d_gain_query = query_pull(d_query_rows)
     key_out, key_pull = jax.vjp(key_part, key_unnormed, gain_key)
-    d_key_raw, d_gain_key = key_pull(rounded(d_keys_own))
+    d_key_raw, d_gain_key = key_pull(d_keys_own)
     d_query_b = d_query_raw.astype(jnp.bfloat16)
     d_key_b = d_key_raw.astype(jnp.bfloat16)
-    d_value_b = d_values_own.astype(jnp.bfloat16)
-    projection_grads = jnp.concatenate([d_query_b, d_key_b, d_value_b], axis=1)
+    projection_grads = jnp.concatenate([d_query_b, d_key_b, d_values_own], axis=1)
     projection_sum = lax.psum_scatter(
-        column_term(normed1, projection_grads),
+        column_term(normed1, projection_grads).astype(jnp.bfloat16),
         ("dp", "seq", "fsdp"),
         scatter_dimension=0,
         tiled=True,
-    )
-    d_normed1 = (
-        contract_cols(d_query_b, query_all)
-        + contract_cols(d_key_b, key_all)
-        + contract_cols(d_value_b, value_all)
-    )
+    ).astype(jnp.float32)
+    d_normed1 = contract_cols(projection_grads, qkv_all)
     norm1_out, norm1_pull = jax.vjp(rms_scale, inputs, gain_one)
     d_input_norm, d_gain_one = norm1_pull(d_normed1)
     gain_sums = lax.psum((d_gain_one, d_gain_two, d_gain_query, d_gain_key), ("dp", "seq", "fsdp"))
     input_grad = (d_middle + d_input_norm).astype(jnp.bfloat16)
-    width_share = MODEL_WIDTH // all_parts
+    width_share = weight_rows
     share_start = lax.axis_index(("dp", "seq", "fsdp")) * width_share
     gain_one_own = lax.dynamic_slice_in_dim(gain_sums[0], share_start, width_share)
     gain_two_own = lax.dynamic_slice_in_dim(gain_sums[1], share_start, width_share)
-    query_cols = QUERY_HEADS * HEAD_SIZE
-    kv_cols = KEY_VALUE_HEADS * HEAD_SIZE
     grad_query = projection_sum[:, :query_cols]
     grad_key = projection_sum[:, query_cols : query_cols + kv_cols]
     grad_value = projection_sum[:, query_cols + kv_cols :]
-    grad_gate = gate_up_sum[:, :FF]
-    grad_up = gate_up_sum[:, FF:]
     return (
         block_out[None],
         input_grad[None],

time: 1540 us -> 928 us (0.60)
  waiting for transfers between devices: 1250 us -> 640 us
  local copies, waits for them, and re-layouts: 22.9 us -> 64.9 us
  matrix products: 133 us -> 99.8 us
  blocking collectives: 84.8 us -> 55.1 us
    reduce_scatter x6 -> x7, waiting for transfers between devices: 834 us -> 435 us  [the longest x1 128 us: body(): lax.psum_scatter(column_term(normed1, projection_grads).astype(jnp.bfloat...]
    all_gather x9 -> x6, waiting for transfers between devices: 413 us -> 195 us  [the longest x1 69.3 us: body(): packed = lax.all_gather(packed, ('dp', 'seq', 'fsdp'), axis=0, tiled=True)]
    unnamed x1 -> x0, blocking collectives: 42 us -> none
    dot_general x4, matrix products: 35.5 us -> 20 us  [contract_rows(): lax.dot_general(left, right, (((0,), (0,)), ((), ())), preferred_element_...]
    dot_general x7 -> x4, matrix products: 34.4 us -> 23 us  [matmul(): return jnp.dot(left, right, preferred_element_type=jnp.float32)]
  transfers between devices with their start and end apart: 15 -> 14, of which waited for: 15 -> 13; matrix products, arithmetic and copies ran while one was open for 9% -> 14% of each run, Pallas kernels for 0% -> 0%
where the time goes in v1:
time: 928 us; the launch traced here: 922 us
  waiting for transfers between devices  640 us (69%)
  matrix products  99.8 us (11%)
  local copies, waits for them, and re-layouts  64.9 us (7%)
  blocking collectives  55.1 us (6%)
  other arithmetic  40.5 us (4%)
  between operations  15.2 us (2%)
    reduce_scatter x1, waiting for transfers between devices, body(): lax.psum_scatter(column_term(normed1, projection_grads).astype(jnp.bfloat...  128 us
    reduce_scatter x1, waiting for transfers between devices, body(): lax.psum_scatter(gate_up_sum, ('dp', 'fsdp'), scatter_dimension=0, tiled=...  94.4 us
    reduce_scatter x1, waiting for transfers between devices, body(): lax.psum_scatter(column_term(attended_b, d_branch).astype(jnp.bfloat16),...  93.1 us
    all_gather x1, waiting for transfers between devices, body(): packed = lax.all_gather(packed, ('dp', 'seq', 'fsdp'), axis=0, tiled=True)  69.3 us
    reduce_scatter x1, waiting for transfers between devices, body(): lax.psum_scatter(column_term(hidden, grad_all).astype(jnp.bfloat16), ('dp...  64 us
    all_gather x1, waiting for transfers between devices, body(): down_all = lax.all_gather(w_down, ('dp', 'fsdp'), axis=0, tiled=True)  54.1 us
    psum x1, blocking collectives, body(): lax.psum((d_gain_one, d_gain_two, d_gain_query, d_gain_key), ('dp', 'seq'...  40.2 us
    all_gather x1, waiting for transfers between devices, body(): lax.all_gather(gate_up.reshape(seq_parts * weight_rows, 2 * units), ('dp'...  40.2 us
  transfers between devices with their start and end apart: 14, of which 13 were waited for; matrix products, arithmetic and copies ran while one was open for 14% of the time, Pallas kernels for 0%

profile of v1, /device:TPU:0, one launch (start us, length us, event | category | flops | bytes accessed | tf_op | source)
XLA Modules:
  0.0 921.6 jit_solution(7887584820192089729)
XLA Ops:
  15.6 69.3 %all-gather.8.cloned.1.call-done = bf16[1024,3200]{1,0:T(8,128)(2,1)} async-done(((bf16[32,3200]{1,0:T(8,128)(2,1)}), bf16[1024,3200]{1,0:T(8,128)(2,1)}) %all-gather.8.cloned.1.call-update) | async-done | bytes 6553616 | tf_op jit(solution)/shard_map/all_gather | solution.py:119
  85.0 2.0 convert_reduce_fusion
  86.9 3.7 fusion.18
  98.1 2.6 reshape.335
  103.2 2.6 reshape.337
  109.4 14.9 %all_to_all.10 = bf16[4,32,2304]{2,1,0:T(8,128)(2,1)} all-to-all(bf16[4,32,2304]{2,1,0:T(8,128)(2,1)S(1)} %pad_maximum_fusion.7), channel_id=1, replica_groups=mesh['dp'=2,'seq'=4,'fsdp'=4] {'seq'}, dimensions={0} | all-to-all | bytes 1179648 | tf_op jit(solution)/shard_map/all_to_all | solution.py:135
  126.8 2.6 copy.101
  136.3 2.5 add_convert_fusion.1
  139.0 3.0 fusion.80
  143.6 2.7 copy.104
  146.2 2.5 fusion.2
  148.8 4.0 fusion.4
  152.8 1.9 copy-done
  154.7 4.7 fusion.54
  159.4 2.6 multiply_reduce_fusion.3
  165.5 40.2 %all-gather.14.cloned.1.call-done = bf16[1024,2304]{1,0:T(8,128)(2,1)} async-done(((bf16[128,2304]{1,0:T(8,128)(2,1)}), bf16[1024,2304]{1,0:T(8,128)(2,1)}) %all-gather.14.cloned.1.call-update) | async-done | bytes 4718608 | tf_op jit(solution)/shard_map/all_gather | solution.py:136
  205.7 4.9 copy.108
  210.6 17.9 %all-gather.12.cloned.1.call-done = bf16[1024,1024]{1,0:T(8,128)(2,1)} async-done(((bf16[256,1024]{1,0:T(8,128)(2,1)}), bf16[1024,1024]{1,0:T(8,128)(2,1)}) %all-gather.12.cloned.1.call-update) | async-done | bytes 2097168 | tf_op jit(solution)/shard_map/all_gather | solution.py:218
  228.5 10.1 %fusion.83 = f32[1024,2304]{1,0:T(8,128)} fusion(bf16[1024,1024]{1,0:T(8,128)(2,1)} %all-gather.12.cloned.1.call-done, bf16[1024,2304]{1,0:T(8,128)(2,1)} %bitcast.171), kind=kOutput, calls=%fused_computation.154 | convolution fusion | flops 4831838208 | bytes 16252928 | tf_op jit(solution)/shard_map/dot_general | solution.py:57
  238.6 14.0 %all-gather.18.cloned.1.call-done = bf16[1,1024,1024]{2,1,0:T(8,128)(2,1)} async-done(((bf16[1,256,1024]{2,1,0:T(8,128)(2,1)}), bf16[1,1024,1024]{2,1,0:T(8,128)(2,1)}) %all-gather.18.cloned.1.call-update) | async-done | bytes 2097168 | tf_op jit(solution)/shard_map/all_gather | solution.py:145
  252.5 54.1 %all-gather.16.cloned.1.call-done = bf16[1152,1024]{1,0:T(8,128)(2,1)} async-done(((bf16[144,1024]{1,0:T(8,128)(2,1)}), bf16[1152,1024]{1,0:T(8,128)(2,1)}) %all-gather.16.cloned.1.call-update) | async-done | bytes 2359312 | tf_op jit(solution)/shard_map/all_gather | solution.py:144
  306.6 10.7 %fusion.14 = (bf16[1024,1152]{1,0:T(8,128)(2,1)S(1)}, bf16[1024,1152]{1,0:T(8,128)(2,1)S(1)}, bf16[1024,1152]{1,0:T(8,128)(2,1)}) fusion(f32[1024,2304]{1,0:T(8,128)} %fusion.83, bf16[1152,1024]{1,0:T(8,128)(2,1)} %all-gather.16.cloned.1.call-done, bf16[1,1024,1024]{2,1,0:T(8,128)(2,1)} %all-gather.18.cloned.1.call-done), kind=kOutput, calls=%fused_computation.18 | convolution fusion | flops 2434793472 | bytes 20971520 | tf_op jit(solution)/shard_map/dot_general | solution.py:67
  319.4 8.6 fusion.25
  328.1 6.6 convolution_convert_fusion.3
  336.4 21.8 %reduce-scatter.10.cloned.1.call-done = bf16[256,1024]{1,0:T(8,128)(2,1)} async-done(((bf16[1024,1024]{1,0:T(8,128)(2,1)}), bf16[256,1024]{1,0:T(8,128)(2,1)}) %reduce-scatter.10.cloned.1.call-update) | async-done | bytes 524304 | tf_op jit(solution)/shard_map/reduce_scatter | solution.py:232
  358.2 2.0 fusion.45
  361.4 30.9 %reduce-scatter.8.cloned.1.call-done = bf16[256,1024]{1,0:T(8,128)(2,1)} async-done(((bf16[1024,1024]{1,0:T(8,128)(2,1)}), bf16[256,1024]{1,0:T(8,128)(2,1)}) %reduce-scatter.8.cloned.1.call-update) | async-done | bytes 524304 | tf_op jit(solution)/shard_map/reduce_scatter | solution.py:234
  392.3 2.6 fusion.48
  395.9 2.4 fusion.35
  399.9 7.7 bitcast_convert_fusion
  407.6 8.9 multiply_convert_fusion
  416.5 2.6 fusion.21
  421.4 6.4 convolution_convert_fusion.1
  428.0 2.1 convolution_convert_fusion.4
  430.4 8.1 convolution_convert_fusion
  438.5 2.6 copy.114
  442.4 4.9 fusion.34
  450.0 3.0 reduce-scatter.12.cloned.1.call-done
  458.2 3.4 convolution_convert_fusion.2
  461.6 64.0 %reduce-scatter.20.cloned.1.call-done = bf16[144,1024]{1,0:T(8,128)(2,1)} async-done(((bf16[1152,1024]{1,0:T(8,128)(2,1)}), bf16[144,1024]{1,0:T(8,128)(2,1)}) %reduce-scatter.20.cloned.1.call-update) | async-done | bytes 294928 | tf_op jit(solution)/shard_map/reduce_scatter | solution.py:238
  525.6 1.8 convert_element_type.235
  527.5 3.8 fusion.43
  531.4 40.2 %all-reduce.4 = (f32[1024]{0:T(1024)S(1)}, f32[64]{0:T(128)}, f32[64]{0:T(128)}, f32[1024]{0:T(1024)S(1)}) all-reduce(f32[1024]{0:T(1024)S(1)} %get-tuple-element.17, f32[64]{0:T(128)S(1)} %copy-done.38, f32[64]{0:T(128)S(1)} %get-tuple-element.21, f32[1024]{0:T(1024)S(1)} %copy-done.27), channel_id=1, replica_groups=mesh['dp'=2,'seq'=4,'fsdp'=4] {'dp','seq','fsdp'}, use_global_device_ids=true, to_apply=%region_17.18 | all-reduce | flops 2176 | bytes 17408 | tf_op jit(solution)/shard_map/psum | solution.py:329
  572.7 93.1 %reduce-scatter.16.cloned.1.call-done = bf16[32,1024]{1,0:T(8,128)(2,1)} async-done(((bf16[1024,1024]{1,0:T(8,128)(2,1)}), bf16[32,1024]{1,0:T(8,128)(2,1)}) %reduce-scatter.16.cloned.1.call-update) | async-done | bytes 65552 | tf_op jit(solution)/shard_map/reduce_scatter | solution.py:268
  667.3 94.4 %reduce-scatter.18.cloned.1.call-done = bf16[128,2304]{1,0:T(8,128)(2,1)} async-done(((bf16[1024,2304]{1,0:T(8,128)(2,1)}), bf16[128,2304]{1,0:T(8,128)(2,1)}) %reduce-scatter.18.cloned.1.call-update) | async-done | bytes 589840 | tf_op jit(solution)/shard_map/reduce_scatter | solution.py:251
  761.7 4.4 all-to-all-start.1
  767.3 8.7 all-to-all-done.1
  784.1 127.5 %reduce-scatter.14.cloned.1.call-done = bf16[32,2048]{1,0:T(8,128)(2,1)} async-done(((bf16[1024,2048]{1,0:T(8,128)(2,1)}), bf16[32,2048]{1,0:T(8,128)(2,1)}) %reduce-scatter.14.cloned.1.call-update) | async-done | bytes 131088 | tf_op jit(solution)/shard_map/reduce_scatter | solution.py:320
  (199 shorter events, 70.5 us)
Async XLA Ops:
  7.2 77.8 %all-gather.8.cloned.1.call-start = ((), (), s32[]{:S(2)}) async-start(), calls=%async_computation.9 | async-start | bytes 6758400 | tf_op jit(solution)/shard_map/all_gather | solution.py:119
  10.4 128.6 %all-gather.10.cloned.1.call-start = ((), (), s32[]{:S(2)}) async-start(), calls=%async_computation.10 | async-start | bytes 2621440 | tf_op jit(solution)/shard_map/all_gather | solution.py:189
  11.1 81.3 %copy-start.33 = (f32[64]{0:T(128)}, f32[64]{0:T(128)S(1)}, u32[]{:S(2)}) copy-start(f32[64]{0:T(128)S(1)} %convert_element_type.187) | copy-start | bytes 772
  15.6 75.9 %copy-start.36 = (f32[256]{0:T(256)}, f32[256]{0:T(256)S(1)}, u32[]{:S(2)}) copy-start(f32[256]{0:T(256)S(1)} %fusion.69) | copy-start | bytes 3076
  86.9 4.5 copy-start.25
  90.6 39.1 %copy-start.7 = (f32[256,2048]{1,0:T(8,128)}, f32[256,2048]{1,0:T(8,128)S(1)}, u32[]{:S(2)}) copy-start(f32[256,2048]{1,0:T(8,128)S(1)} %fusion.18) | copy-start | bytes 6291460
  92.4 5.7 copy-start.18
  96.2 28.6 %copy-start.39 = (bf16[64]{0:T(256)(128)(2,1)S(1)}, bf16[64]{0:T(256)(128)(2,1)}, u32[]{:S(2)}) copy-start(bf16[64]{0:T(256)(128)(2,1)} %param.24) | copy-start | bytes 388
  96.2 28.6 %copy-start.40 = (s32[1,4]{1,0:T(1,128)S(1)}, s32[1,4]{1,0:T(1,128)}, u32[]{:S(2)}) copy-start(s32[1,4]{1,0:T(1,128)} %param.17) | copy-start | bytes 52
  98.1 107.6 %all-gather.14.cloned.1.call-start = ((), (), s32[]{:S(2)}) async-start(), calls=%async_computation.12 | async-start | bytes 5308416 | tf_op jit(solution)/shard_map/all_gather | solution.py:136
  124.3 104.2 %all-gather.12.cloned.1.call-start = ((), (), s32[]{:S(2)}) async-start(), calls=%async_computation.11 | async-start | bytes 2621440 | tf_op jit(solution)/shard_map/all_gather | solution.py:218
  124.9 8.3 copy-start.34
  143.5 5.2 copy-start.2
  148.7 4.1 copy-start.21
  148.8 6.0 copy-start
  148.8 5.9 copy-start.13
  152.8 6.6 copy-start.22
  154.7 4.7 copy-start.8
  154.7 8.4 copy-start.24
  159.4 2.6 copy-start.11
  164.1 88.4 %all-gather.18.cloned.1.call-start = ((), (), s32[]{:S(2)}) async-start(), calls=%async_computation.21 | async-start | bytes 2621440 | tf_op jit(solution)/shard_map/all_gather | solution.py:145
  164.7 141.9 %all-gather.16.cloned.1.call-start = ((), (), s32[]{:S(2)}) async-start(), calls=%async_computation.13 | async-start | bytes 2654208 | tf_op jit(solution)/shard_map/all_gather | solution.py:144
  165.3 192.9 %reduce-scatter.10.cloned.1.call-start = ((), (), s32[]{:S(2)}) async-start(), calls=%async_computation.15 | async-start | bytes 2621440 | tf_op jit(solution)/shard_map/reduce_scatter | solution.py:232
  317.3 2.2 copy-start.42
  328.1 64.3 %reduce-scatter.8.cloned.1.call-start = ((), (), s32[]{:S(2)}) async-start(), calls=%async_computation.14 | async-start | bytes 2621440 | tf_op jit(solution)/shard_map/reduce_scatter | solution.py:234
  334.8 118.2 %reduce-scatter.12.cloned.1.call-start = ((), (), s32[]{:S(2)}) async-start(), calls=%async_computation.16 | async-start | bytes 2621440 | tf_op jit(solution)/shard_map/reduce_scatter | solution.py:302
  399.8 7.7 copy-start.14
  399.9 7.7 copy-start.28
  416.4 3.3 copy-start.1
  421.4 6.6 copy-start.5
  421.4 6.6 copy-start.12
  421.4 104.3 %reduce-scatter.20.cloned.1.call-start = ((), (), s32[]{:S(2)}) async-start(), calls=%async_computation.20 | async-start | bytes 2654208 | tf_op jit(solution)/shard_map/reduce_scatter | solution.py:238
  427.9 237.9 %reduce-scatter.16.cloned.1.call-start = ((), (), s32[]{:S(2)}) async-start(), calls=%async_computation.18 | async-start | bytes 2162688 | tf_op jit(solution)/shard_map/reduce_scatter | solution.py:268
  430.1 331.6 %reduce-scatter.18.cloned.1.call-start = ((), (), s32[]{:S(2)}) async-start(), calls=%async_computation.19 | async-start | bytes 5308416 | tf_op jit(solution)/shard_map/reduce_scatter | solution.py:251
  441.2 6.4 copy-start.35
  441.2 470.5 %reduce-scatter.14.cloned.1.call-start = ((), (), s32[]{:S(2)}) async-start(), calls=%async_computation.17 | async-start | bytes 4325376 | tf_op jit(solution)/shard_map/reduce_scatter | solution.py:320
  448.7 9.4 %copy-start.9 = (bf16[1,256,1024]{2,1,0:T(8,128)(2,1)S(1)}, bf16[1,256,1024]{2,1,0:T(8,128)(2,1)}, u32[]{:S(2)}) copy-start(bf16[1,256,1024]{2,1,0:T(8,128)(2,1)} %param.15) | copy-start | bytes 1572868
  450.0 8.2 copy-start.15
  450.0 8.2 copy-start.26
  450.0 8.2 copy-start.37
  452.9 4.2 copy-start.10
  458.1 3.5 copy-start.17
  458.1 69.3 %copy-start.16 = (bf16[256,16,64]{0,2,1:T(8,128)(2,1)S(1)}, bf16[256,16,64]{0,2,1:T(8,128)(2,1)}, u32[]{:S(2)}) copy-start(bf16[256,16,64]{0,2,1:T(8,128)(2,1)} %fusion.49) | copy-start | bytes 1572868
  527.5 3.9 copy-start.27
  527.5 3.9 copy-start.38
  527.5 238.7 %copy-start.31 = (f32[256]{0:T(256)S(1)}, f32[256]{0:T(256)}, u32[]{:S(2)}) copy-start(f32[256]{0:T(256)} %copy-done.30) | copy-start | bytes 3076
  527.5 238.7 %copy-start.6 = (f32[256,1024]{1,0:T(8,128)S(1)}, f32[256,1024]{1,0:T(8,128)}, u32[]{:S(2)}) copy-start(f32[256,1024]{1,0:T(8,128)} %copy-done.4) | copy-start | bytes 3145732
  761.7 14.3 %all-to-all-start.1 = ((bf16[4,32,2304]{2,1,0:T(8,128)(2,1)}), bf16[4,32,2304]{2,1,0:T(8,128)(2,1)}, u32[]{:S(2)}, u32[]{:S(2)}) async-start(bf16[4,32,2304]{2,1,0:T(8,128)(2,1)} %bitcast.193), calls=%async_computation.7 | async-start | bytes 1179648 | tf_op jit(solution)/shard_map/all_to_all | solution.py:252
  (9 other events, 8.0 us)
Sparse Core Ops, SparseCore 0:
  11.4 73.4 all-gather.7
  98.2 23.3 all-gather.9
  124.4 81.2 all-gather.13
  207.7 20.7 all-gather.11
  229.9 22.5 all-gather.17
  254.5 52.0 all-gather.15
  328.2 29.9 reduce-scatter.9
  360.9 31.4 reduce-scatter.7
  421.5 31.4 reduce-scatter.11
  456.7 68.9 reduce-scatter.19
  528.0 137.7 reduce-scatter.15
  669.3 92.3 reduce-scatter.17
  764.0 147.6 reduce-scatter.13

commit v2 on v1

--- a/solution.py
+++ b/solution.py
@@ -67,6 +67,37 @@
     return lax.dot_general(
         left, right, (((1,), (1,)), ((), ())), preferred_element_type=jnp.float32
     )
+
+
+def exchange(blocks, bit, parts):
+    pairs = [(place, place ^ bit) for place in range(parts)]
+    received = lax.ppermute(jnp.concatenate(blocks, axis=0), "seq", pairs)
+    return jnp.split(received, len(blocks), axis=0)
+
+
+def gather_seq(own):
+    parts = lax.axis_size("seq")
+    blocks = {0: own}
+    bit = parts // 2
+    while bit:
+        keys = sorted(blocks)
+        for key, block in zip(keys, exchange([blocks[key] for key in keys], bit, parts)):
+            blocks[key ^ bit] = block
+        bit //= 2
+    return [blocks[key] for key in range(parts)]
+
+
+def scatter_seq(blocks):
+    parts = lax.axis_size("seq")
+    held = {key: block.astype(jnp.float32) for key, block in enumerate(blocks)}
+    bit = 1
+    while bit < parts:
+        keys = [key for key in sorted(held) if key & bit]
+        sent = [held.pop(key).astype(jnp.bfloat16) for key in keys]
+        for key, block in zip(keys, exchange(sent, bit, parts)):
+            held[key ^ bit] = held[key ^ bit] + block.astype(jnp.float32)
+        bit *= 2
+    return held[0]
 
 
 def column_term(left, right):
@@ -117,22 +148,23 @@
         axis=1,
     )
     packed = lax.all_gather(packed, ("dp", "seq", "fsdp"), axis=0, tiled=True)
+
+    dp_parts = lax.axis_size("dp")
+    fsdp_parts = lax.axis_size("fsdp")
+    unit_rows = w_down.shape[0]
+    units = dp_parts * fsdp_parts * unit_rows
+
+    def by_owner(columns):
+        split = columns.reshape(weight_rows, dp_parts, seq_parts, fsdp_parts, unit_rows)
+        return split.transpose(2, 0, 1, 3, 4).reshape(seq_parts, weight_rows, units)
+
+    gate_up = jnp.concatenate([by_owner(w_gate), by_owner(w_up)], axis=2)
+    gate_up = lax.all_to_all(gate_up, "seq", 0, 0)
+    packed, gate_up = lax.optimization_barrier((packed, gate_up))
     qkv_all = packed[:, :qkv_cols]
     out_all = packed[:, qkv_cols : qkv_cols + MODEL_WIDTH]
     norm1_all = packed[:, qkv_cols + MODEL_WIDTH]
     norm2_all = packed[:, qkv_cols + MODEL_WIDTH + 1]
-
-    dp_parts = lax.axis_size("dp")
-    fsdp_parts = lax.axis_size("fsdp")
-    unit_rows = w_down.shape[0]
-    units = dp_parts * fsdp_parts * unit_rows
-
-    def by_owner(columns):
-        split = columns.reshape(weight_rows, dp_parts, seq_parts, fsdp_parts, unit_rows)
-        return split.transpose(2, 0, 1, 3, 4).reshape(seq_parts, weight_rows, units)
-
-    gate_up = jnp.concatenate([by_owner(w_gate), by_owner(w_up)], axis=2)
-    gate_up = lax.all_to_all(gate_up, "seq", 0, 0)
     gate_up = lax.all_gather(
         gate_up.reshape(seq_parts * weight_rows, 2 * units), ("dp", "fsdp"), axis=0, tiled=True
     )
@@ -142,7 +174,7 @@
         .reshape(MODEL_WIDTH, 2 * units)
     )
     down_all = lax.all_gather(w_down, ("dp", "fsdp"), axis=0, tiled=True)
-    grad_all = lax.all_gather(out_grad[0], "seq", axis=0, tiled=True)
+    grad_all = jnp.concatenate(gather_seq(out_grad[0]), axis=0)
     inputs = tokens[0].astype(jnp.float32)
     gain_one = norm1_all.astype(jnp.float32)
     normed1 = rms_scale(inputs, gain_one).astype(jnp.bfloat16)
@@ -176,8 +208,15 @@
             )
             * score_scale
         )
-        key_places = jnp.arange(total_amount, dtype=jnp.int32)
-        allowed = (own_segments[:, None] == segments[None, :]) & (
+        key_places = jnp.concatenate(
+            [
+                (my_index ^ part) * token_rows + jnp.arange(token_rows, dtype=jnp.int32)
+                for part in range(seq_parts)
+            ]
+        )
+        doc_ends = jnp.cumsum(doc_lengths[0])
+        key_segments = jnp.sum((key_places[:, None] >= doc_ends[None, :]).astype(jnp.int32), axis=1)
+        allowed = (own_segments[:, None] == key_segments[None, :]) & (
             own_places[:, None] >= key_places[None, :]
         )
         return (scores, allowed, key_three_axes)
@@ -186,8 +225,8 @@
         (KEY_VALUE_HEADS, queries_per_group, token_rows), masked_fill_value, jnp.float32
     )
     row_top = starting_maximum
-    both_rows = lax.all_gather(
-        jnp.concatenate([key_rows, value_rows], axis=1), "seq", axis=0, tiled=True
+    both_rows = jnp.concatenate(
+        gather_seq(jnp.concatenate([key_rows, value_rows], axis=1)), axis=0
     )
     key_rows_part = both_rows[:, :kv_cols]
     value_rows_part = both_rows[:, kv_cols:]
@@ -215,7 +254,7 @@
     middle = inputs + matmul(attended_b, out_all)
     gain_two = norm2_all.astype(jnp.float32)
     normed2 = rms_scale(middle, gain_two).astype(jnp.bfloat16)
-    normed2_all = lax.all_gather(normed2, "seq", axis=0, tiled=True)
+    normed2_all = jnp.concatenate(gather_seq(normed2), axis=0)
     gate_up_pre = matmul(normed2_all, gate_up)
     gate_pre = gate_up_pre[:, :units]
     up_pre = gate_up_pre[:, units:]
@@ -228,19 +267,11 @@
     d_hidden = contract_cols(grad_all, down_all)
     d_gate, d_up = swiglu_pull(d_hidden)
     gate_up_grads = jnp.concatenate([d_gate.astype(jnp.bfloat16), d_up.astype(jnp.bfloat16)], axis=1)
-    d_normed2 = contract_cols(gate_up_grads, gate_up).astype(jnp.bfloat16)
-    d_normed2 = lax.psum_scatter(d_normed2, "seq", scatter_dimension=0, tiled=True)
-    d_normed2 = d_normed2.astype(jnp.float32)
-    branch = lax.psum_scatter(
-        matmul(hidden, down_all).astype(jnp.bfloat16), "seq", scatter_dimension=0, tiled=True
-    )
-    block_out = (middle + branch.astype(jnp.float32)).astype(jnp.bfloat16)
-    down_sum = lax.psum_scatter(
-        column_term(hidden, grad_all).astype(jnp.bfloat16),
-        ("dp", "fsdp"),
-        scatter_dimension=0,
-        tiled=True,
-    ).astype(jnp.float32)
+    d_normed2 = contract_cols(gate_up_grads, gate_up)
+    d_normed2 = scatter_seq(jnp.split(d_normed2, seq_parts, axis=0))
+    branch = scatter_seq(jnp.split(matmul(hidden, down_all), seq_parts, axis=0))
+    block_out = (middle + branch).astype(jnp.bfloat16)
+    down_sum = column_term(hidden, grad_all).astype(jnp.bfloat16)
     gate_up_sum = (
         column_term(normed2_all, gate_up_grads)
         .astype(jnp.bfloat16)
@@ -248,6 +279,10 @@
         .transpose(0, 2, 1, 3, 4)
         .reshape(MODEL_WIDTH, 2 * units)
     )
+    d_normed2, down_sum, gate_up_sum = lax.optimization_barrier((d_normed2, down_sum, gate_up_sum))
+    down_sum = lax.psum_scatter(
+        down_sum, ("dp", "fsdp"), scatter_dimension=0, tiled=True
+    ).astype(jnp.float32)
     gate_up_sum = lax.psum_scatter(gate_up_sum, ("dp", "fsdp"), scatter_dimension=0, tiled=True)
     gate_up_sum = lax.all_to_all(
         gate_up_sum.reshape(seq_parts, weight_rows, 2 * units), "seq", 0, 0
@@ -265,12 +300,6 @@
     d_middle_norm, d_gain_two = norm2_pull(d_normed2)
     d_middle = grad_float + d_middle_norm
     d_branch = d_middle.astype(jnp.bfloat16)
-    out_sum = lax.psum_scatter(
-        column_term(attended_b, d_branch).astype(jnp.bfloat16),
-        ("dp", "seq", "fsdp"),
-        scatter_dimension=0,
-        tiled=True,
-    ).astype(jnp.float32)
     attended_gradient = contract_cols(d_branch, out_all).astype(jnp.bfloat16)
     attended_grad_four = attended_gradient.reshape(
         token_rows, KEY_VALUE_HEADS, queries_per_group, HEAD_SIZE
@@ -299,12 +328,11 @@
     )
     every_key_gradient = local_key_gradient.reshape(total_amount, KEY_VALUE_HEADS * HEAD_SIZE)
     every_value_gradient = value_gradient.reshape(total_amount, KEY_VALUE_HEADS * HEAD_SIZE)
-    d_both_own = lax.psum_scatter(
-        jnp.concatenate([every_key_gradient, every_value_gradient], axis=1).astype(jnp.bfloat16),
-        "seq",
-        scatter_dimension=0,
-        tiled=True,
-    )
+    d_both_own = scatter_seq(
+        jnp.split(
+            jnp.concatenate([every_key_gradient, every_value_gradient], axis=1), seq_parts, axis=0
+        )
+    ).astype(jnp.bfloat16)
     d_keys_own = d_both_own[:, :kv_cols].astype(jnp.float32)
     d_values_own = d_both_own[:, kv_cols:]
     d_query_rows = rounded(
@@ -317,15 +345,31 @@
     d_query_b = d_query_raw.astype(jnp.bfloat16)
     d_key_b = d_key_raw.astype(jnp.bfloat16)
     projection_grads = jnp.concatenate([d_query_b, d_key_b, d_values_own], axis=1)
-    projection_sum = lax.psum_scatter(
-        column_term(normed1, projection_grads).astype(jnp.bfloat16),
-        ("dp", "seq", "fsdp"),
-        scatter_dimension=0,
-        tiled=True,
-    ).astype(jnp.float32)
+    attention_sum = jnp.concatenate(
+        [column_term(normed1, projection_grads), column_term(attended_b, d_branch)], axis=1
+    ).astype(jnp.bfloat16)
+    attention_cols = attention_sum.shape[1]
+    attention_sum = attention_sum.reshape(
+        dp_parts, seq_parts, fsdp_parts * weight_rows, attention_cols
+    )
+    attention_sum = scatter_seq(
+        [
+            lax.dynamic_index_in_dim(attention_sum, my_index ^ part, axis=1, keepdims=False)
+            for part in range(seq_parts)
+        ]
+    ).astype(jnp.bfloat16)
+    attention_sum = attention_sum.reshape(dp_parts * fsdp_parts * weight_rows, attention_cols)
     d_normed1 = contract_cols(projection_grads, qkv_all)
     norm1_out, norm1_pull = jax.vjp(rms_scale, inputs, gain_one)
     d_input_norm, d_gain_one = norm1_pull(d_normed1)
+    attention_sum, d_gain_one, d_gain_two, d_gain_query, d_gain_key = lax.optimization_barrier(
+        (attention_sum, d_gain_one, d_gain_two, d_gain_query, d_gain_key)
+    )
+    attention_sum = lax.psum_scatter(
+        attention_sum, ("dp", "fsdp"), scatter_dimension=0, tiled=True
+    ).astype(jnp.float32)
+    projection_sum = attention_sum[:, :qkv_cols]
+    out_sum = attention_sum[:, qkv_cols:]
     gain_sums = lax.psum((d_gain_one, d_gain_two, d_gain_query, d_gain_key), ("dp", "seq", "fsdp"))
     input_grad = (d_middle + d_input_norm).astype(jnp.bfloat16)
     width_share = weight_rows

time: 928 us -> 530 us (0.57)
  waiting for transfers between devices: 640 us -> 198 us
  other arithmetic: 40.5 us -> 62.7 us
  local copies, waits for them, and re-layouts: 64.9 us -> 81.3 us
    reduce_scatter x6 -> x2, waiting for transfers between devices: 340 us -> 42.6 us  [the longest x1 42.6 us: body(): lax.psum_scatter(attention_sum, ('dp', 'fsdp'), scatter_dimension=0, tile...]
    reduce_scatter x1, waiting for transfers between devices: 94.4 us -> 0.01 us  [body(): lax.psum_scatter(gate_up_sum, ('dp', 'fsdp'), scatter_dimension=0, tiled=...]
    ppermute x0 -> x14, waiting for transfers between devices: none -> 81.8 us  [exchange(): received = lax.ppermute(jnp.concatenate(blocks, axis=0), 'seq', pairs)]
    all_gather x1, waiting for transfers between devices: 40.2 us -> 0.01 us  [body(): lax.all_gather(gate_up.reshape(seq_parts * weight_rows, 2 * units), ('dp'...]
    all_gather x1, waiting for transfers between devices: 54.1 us -> 18.6 us  [body(): down_all = lax.all_gather(w_down, ('dp', 'fsdp'), axis=0, tiled=True)]
    all_gather x3 -> x0, waiting for transfers between devices: 31.9 us -> none  [the longest x1 17.9 us: body(): normed2_all = lax.all_gather(normed2, 'seq', axis=0, tiled=True)]
    all_gather x1, waiting for transfers between devices: 69.3 us -> 55.3 us  [body(): packed = lax.all_gather(packed, ('dp', 'seq', 'fsdp'), axis=0, tiled=True)]
    convert_element_type x2 -> x7, other arithmetic: 3.34 us -> 15.7 us  [the longest x4 7.99 us: scatter_seq(): sent = [held.pop(key).astype(jnp.bfloat16) for key in keys]]
  transfers between devices with their start and end apart: 14 -> 21, of which waited for: 13 -> 10; matrix products, arithmetic and copies ran while one was open for 14% -> 39% of each run, Pallas kernels for 0% -> 0%
where the time goes in v2:
time: 530 us; the launch traced here: 520 us
  waiting for transfers between devices  198 us (37%)
  matrix products  96 us (18%)
  local copies, waits for them, and re-layouts  81.3 us (15%)
  other arithmetic  62.7 us (12%)
  blocking collectives  54.6 us (10%)
  between operations  15.8 us (3%)
  starting transfers between devices  11.6 us (2%)
    ppermute x14, waiting for transfers between devices, exchange(): received = lax.ppermute(jnp.concatenate(blocks, axis=0), 'seq', pairs)  81.8 us
    all_gather x1, waiting for transfers between devices, body(): packed = lax.all_gather(packed, ('dp', 'seq', 'fsdp'), axis=0, tiled=True)  55.3 us
    reduce_scatter x1, waiting for transfers between devices, body(): lax.psum_scatter(attention_sum, ('dp', 'fsdp'), scatter_dimension=0, tile...  42.6 us
    psum x1, blocking collectives, body(): lax.psum((d_gain_one, d_gain_two, d_gain_query, d_gain_key), ('dp', 'seq'...  39.5 us
    dot_general x4, matrix products, contract_cols(): lax.dot_general(left, right, (((1,), (1,)), ((), ())), preferred_element_...  23.2 us
    dot_general x4, matrix products, matmul(): return jnp.dot(left, right, preferred_element_type=jnp.float32)  19.7 us
    all_gather x1, waiting for transfers between devices, body(): down_all = lax.all_gather(w_down, ('dp', 'fsdp'), axis=0, tiled=True)  18.6 us
    dot_general x4, matrix products, contract_rows(): lax.dot_general(left, right, (((0,), (0,)), ((), ())), preferred_element_...  17.3 us
  transfers between devices with their start and end apart: 21, of which 10 were waited for; matrix products, arithmetic and copies ran while one was open for 39% of the time, Pallas kernels for 0%

profile of v2, /device:TPU:0, one launch (start us, length us, event | category | flops | bytes accessed | tf_op | source)
XLA Modules:
  0.0 520.5 jit_solution(15871044499806472756)
XLA Ops:
  15.6 15.2 %all_to_all.10 = bf16[4,32,2304]{2,1,0:T(8,128)(2,1)} all-to-all(bf16[4,32,2304]{2,1,0:T(8,128)(2,1)S(1)} %pad_maximum_fusion.15), channel_id=1, replica_groups=mesh['dp'=2,'seq'=4,'fsdp'=4] {'seq'}, dimensions={0} | all-to-all | bytes 1179648 | tf_op jit(solution)/shard_map/all_to_all | solution.py:162
  30.8 55.3 %all-gather.4.cloned.1.call-done = bf16[1024,3200]{1,0:T(8,128)(2,1)} async-done(((bf16[32,3200]{1,0:T(8,128)(2,1)}), bf16[1024,3200]{1,0:T(8,128)(2,1)}) %all-gather.4.cloned.1.call-update) | async-done | bytes 6553616 | tf_op jit(solution)/shard_map/all_gather | solution.py:150
  96.1 3.5 fusion.19
  116.1 9.0 %collective-permute-done = bf16[256,1024]{1,0:T(8,128)(2,1)} collective-permute-done((bf16[256,1024]{1,0:T(8,128)(2,1)}, bf16[256,1024]{1,0:T(8,128)(2,1)}, u32[]{:S(2)}, u32[]{:S(2)}) %collective-permute-start) | collective-permute-done | bytes 524320 | tf_op jit(solution)/shard_map/ppermute | solution.py:74
  125.1 2.2 pad_maximum_fusion.8
  129.4 2.6 copy.120
  133.0 2.6 copy.118
  135.6 3.1 add_convert_fusion
  145.7 2.6 copy.122
  148.4 2.5 fusion.2
  151.0 4.0 fusion.4
  156.9 4.7 fusion.69
  161.6 2.6 multiply_reduce_fusion.5
  165.8 2.3 pad_maximum_fusion.11
  168.3 10.8 %collective-permute-done.2 = bf16[256,1024]{1,0:T(8,128)(2,1)S(1)} collective-permute-done((bf16[256,1024]{1,0:T(8,128)(2,1)S(1)}, bf16[256,1024]{1,0:T(8,128)(2,1)S(1)}, u32[]{:S(2)}, u32[]{:S(2)}) %collective-permute-start.2) | collective-permute-done | bytes 524320 | tf_op jit(solution)/shard_map/ppermute | solution.py:74
  180.3 2.3 fusion.102
  183.9 2.2 fusion.103
  186.2 2.9 copy.124
  189.1 2.2 copy-done.12
  191.3 9.1 %fusion.75 = f32[1024,2304]{1,0:T(8,128)} fusion(bf16[1024,2304]{1,0:T(8,128)(2,1)S(1)} %bitcast.192, bf16[256,1024]{1,0:T(8,128)(2,1)S(1)} %copy-done.38, bf16[256,1024]{1,0:T(8,128)(2,1)S(1)} %copy-done.32, bf16[256,1024]{1,0:T(8,128)(2,1)S(1)} %copy-done.36, bf16[256,1024]{1,0:T(8,128)(2,1)S(1)} %copy-done.23), kind=kOutput, calls=%fused_computation.154 | convolution fusion | flops 4840226816 | bytes 16252928 | tf_op jit(solution)/shard_map/dot_general | solution.py:57
  200.4 18.6 %all-gather.8.cloned.1.call-done = bf16[1152,1024]{1,0:T(8,128)(2,1)} async-done(((bf16[144,1024]{1,0:T(8,128)(2,1)}), bf16[1152,1024]{1,0:T(8,128)(2,1)}) %all-gather.8.cloned.1.call-update) | async-done | bytes 2359312 | tf_op jit(solution)/shard_map/all_gather | solution.py:176
  219.0 10.7 %fusion.14 = (bf16[1024,1152]{1,0:T(8,128)(2,1)S(1)}, bf16[1024,1152]{1,0:T(8,128)(2,1)S(1)}, bf16[1024,1152]{1,0:T(8,128)(2,1)S(1)}) fusion(f32[1024,2304]{1,0:T(8,128)} %fusion.75, bf16[1152,1024]{1,0:T(8,128)(2,1)} %all-gather.8.cloned.1.call-done, bf16[256,1024]{1,0:T(8,128)(2,1)} %get-tuple-element.68, bf16[256,1024]{1,0:T(8,128)(2,1)} %collective-permute-done.6, ...), kind=kOutput, calls=%fused_computation.31 | convolution fusion | flops 2443182080 | bytes 20971520 | tf_op jit(solution)/shard_map/dot_general | solution.py:67
  229.7 4.5 fusion.108
  235.3 5.1 fusion.107
  242.9 7.8 %convolution_convert_fusion = bf16[1024,2304]{1,0:T(8,128)(2,1)} fusion(bf16[1024,1152]{1,0:T(8,128)(2,1)S(1)} %get-tuple-element.51, bf16[1024,1152]{1,0:T(8,128)(2,1)S(1)} %get-tuple-element.50, bf16[256,1024]{1,0:T(8,128)(2,1)S(1)} %copy-done.39, bf16[256,1024]{1,0:T(8,128)(2,1)S(1)} %copy-done.33, bf16[256,1024]{1,0:T(8,128)(2,1)S(1)} %copy-done.37, ...), kind=kOutput, calls=%fused_computation.28 | convolution fusion | flops 4852023296 | bytes 11534336 | tf_op jit(solution)/shard_map/dot_general | solution.py:61
  253.4 5.3 %convolution_convert_fusion.2 = bf16[1152,1024]{1,0:T(8,128)(2,1)} fusion(bf16[1024,1152]{1,0:T(8,128)(2,1)S(1)} %get-tuple-element.52, bf16[256,1024]{1,0:T(8,128)(2,1)S(1)} %copy-done.35, bf16[256,1024]{1,0:T(8,128)(2,1)} %collective-permute-done.6, bf16[256,1024]{1,0:T(8,128)(2,1)S(1)} %copy-done.34, bf16[256,1024]{1,0:T(8,128)(2,1)} %bitcast.33), kind=kOutput, calls=%fused_computation.39 | convolution fusion | flops 2425487360 | bytes 6815744 | tf_op jit(solution)/shard_map/dot_general | solution.py:61
  258.7 5.0 copy.125
  263.7 2.3 fusion.64
  266.6 2.6 fusion.63
  269.3 2.1 multiply_reduce_fusion.1
  272.0 8.3 %collective-permute-done.5 = bf16[256,1024]{1,0:T(8,128)(2,1)S(1)} collective-permute-done((bf16[256,1024]{1,0:T(8,128)(2,1)}, bf16[256,1024]{1,0:T(8,128)(2,1)S(1)}, u32[]{:S(2)}, u32[]{:S(2)}) %collective-permute-start.5) | collective-permute-done | bytes 524320 | tf_op jit(solution)/shard_map/ppermute | solution.py:74
  280.3 3.1 fusion.49
  284.4 3.2 fusion.40
  290.5 8.9 %multiply_convert_fusion = bf16[8,2,256,1024]{2,3,1,0:T(8,128)(2,1)S(1)} fusion(f32[8,1024,256,2]{2,1,3,0:T(8,128)} %copy-done, bf16[8,2,256,64]{2,3,1,0:T(8,128)(2,1)S(1)} %bitcast.203, bf16[1024,8,64,1]{0,2,3,1:T(8,128)(2,1)S(1)} %bitcast.214, f32[8,2,256]{2,1,0:T(2,128)S(1)} %multiply_reduce_fusion.3, f32[8,2,256]{2,1,0:T(2,128)} %log_add_fusion, ...), kind=kOutput, calls=%fused_computation.4 | convolution fusion | flops 562036736 | bytes 27033600 | tf_op jit(solution)/shard_map/hgqd,khd->hgqk/dot_general | solution.py:317
  299.4 4.0 bitcast_multiply_fusion
  305.4 6.9 %fusion.39 = bf16[8,2,256,64]{2,3,1,0:T(8,128)(2,1)} fusion(bf16[1024,8,64,1]{0,2,3,1:T(8,128)(2,1)} %bitcast.186, bf16[8,2,256,1024]{2,3,1,0:T(8,128)(2,1)} %copy-done.1), kind=kOutput, calls=%fused_computation.79 | convolution fusion | flops 537395200 | bytes 9961472 | tf_op jit(solution)/shard_map/hgqk,khd->hgqd/dot_general | solution.py:322
  312.3 8.9 %fusion.6 = f32[8,64,1024,1]{2,1,3,0:T(8,128)} fusion(bf16[8,2,256,64]{2,3,1,0:T(8,128)(2,1)S(1)} %bitcast.204, f32[8,1024,256,2]{2,1,3,0:T(8,128)} %copy-done, f32[8,2,256]{2,1,0:T(2,128)S(1)} %copy-done.53, pred[256,1024]{0,1:T(8,128)(4,1)S(1)} %compare_and_fusion), kind=kOutput, calls=%fused_computation.14 | convolution fusion | flops 553648128 | bytes 19677184 | tf_op jit(solution)/shard_map/hgqk,hgqd->khd/dot_general | solution.py:311
  321.1 3.1 copy.132
  334.1 10.3 %collective-permute-done.11 = bf16[256,1024]{1,0:T(8,128)(2,1)} collective-permute-done((bf16[256,1024]{1,0:T(8,128)(2,1)}, bf16[256,1024]{1,0:T(8,128)(2,1)}, u32[]{:S(2)}, u32[]{:S(2)}) %collective-permute-start.11) | collective-permute-done | bytes 524320 | tf_op jit(solution)/shard_map/ppermute | solution.py:74
  350.6 4.2 fusion.46
  357.1 2.4 convolution_convert_fusion.1
  363.5 6.0 %collective-permute-done.12 = bf16[4,128,3072]{2,1,0:T(8,128)(2,1)} collective-permute-done((bf16[4,128,3072]{2,1,0:T(8,128)(2,1)}, bf16[4,128,3072]{2,1,0:T(8,128)(2,1)}, u32[]{:S(2)}, u32[]{:S(2)}) %collective-permute-start.12) | collective-permute-done | bytes 3145760 | tf_op jit(solution)/shard_map/ppermute | solution.py:74
  369.5 3.5 fusion.21
  373.5 36.2 %collective-permute-done.13 = bf16[2,128,3072]{2,1,0:T(8,128)(2,1)} collective-permute-done((bf16[2,128,3072]{2,1,0:T(8,128)(2,1)}, bf16[2,128,3072]{2,1,0:T(8,128)(2,1)}, u32[]{:S(2)}, u32[]{:S(2)}) %collective-permute-start.13) | collective-permute-done | bytes 1572896 | tf_op jit(solution)/shard_map/ppermute | solution.py:74
  409.8 4.1 fusion.23
  415.8 39.5 %all-reduce.4 = (f32[1024]{0:T(1024)S(1)}, f32[64]{0:T(128)}, f32[64]{0:T(128)}, f32[1024]{0:T(1024)S(1)}) all-reduce(f32[1024]{0:T(1024)S(1)} %get-tuple-element.26, f32[64]{0:T(128)S(1)} %copy-done.64, f32[64]{0:T(128)S(1)} %get-tuple-element.29, f32[1024]{0:T(1024)S(1)} %copy-done.52), channel_id=1, replica_groups=mesh['dp'=2,'seq'=4,'fsdp'=4] {'dp','seq','fsdp'}, use_global_device_ids=true, to_apply=%region_18.19 | all-reduce | flops 2176 | bytes 17408 | tf_op jit(solution)/shard_map/psum | solution.py:373
  456.4 4.0 all-to-all-start.1
  460.4 42.6 %reduce-scatter.4.cloned.1.call-done = bf16[32,3072]{1,0:T(8,128)(2,1)} async-done(((bf16[256,3072]{1,0:T(8,128)(2,1)}), bf16[32,3072]{1,0:T(8,128)(2,1)}) %reduce-scatter.4.cloned.1.call-update) | async-done | bytes 196624 | tf_op jit(solution)/shard_map/reduce_scatter | solution.py:368
  (289 shorter events, 99.8 us)
Async XLA Ops:
  7.2 78.9 %all-gather.4.cloned.1.call-start = ((), (), s32[]{:S(2)}) async-start(), calls=%async_computation.5 | async-start | bytes 6758400 | tf_op jit(solution)/shard_map/all_gather | solution.py:150
  10.4 77.4 %copy-start.67 = (bf16[64]{0:T(256)(128)(2,1)S(1)}, bf16[64]{0:T(256)(128)(2,1)}, u32[]{:S(2)}) copy-start(bf16[64]{0:T(256)(128)(2,1)} %param.24) | copy-start | bytes 388
  10.4 77.9 %copy-start.66 = (bf16[64]{0:T(256)(128)(2,1)S(1)}, bf16[64]{0:T(256)(128)(2,1)}, u32[]{:S(2)}) copy-start(bf16[64]{0:T(256)(128)(2,1)} %param.25) | copy-start | bytes 388
  10.5 77.9 %copy-start.69 = (s32[1,4]{1,0:T(1,128)S(1)}, s32[1,4]{1,0:T(1,128)}, u32[]{:S(2)}) copy-start(s32[1,4]{1,0:T(1,128)} %param.17) | copy-start | bytes 52
  10.5 78.1 %copy-start.14 = (bf16[1,256,1024]{2,1,0:T(8,128)(2,1)S(1)}, bf16[1,256,1024]{2,1,0:T(8,128)(2,1)}, u32[]{:S(2)}) copy-start(bf16[1,256,1024]{2,1,0:T(8,128)(2,1)} %param.15) | copy-start | bytes 1572868
  10.5 175.7 %all-gather.6.cloned.1.call-start = ((), (), s32[]{:S(2)}) async-start(), calls=%async_computation.6 | async-start | bytes 5308416 | tf_op jit(solution)/shard_map/all_gather | solution.py:168
  12.4 76.3 %copy-start.65 = (s32[1,256]{1,0:T(1,128)S(1)}, s32[1,256]{1,0:T(1,128)}, u32[]{:S(2)}) copy-start(s32[1,256]{1,0:T(1,128)} %param.18) | copy-start | bytes 3076
  86.1 132.8 %all-gather.8.cloned.1.call-start = ((), (), s32[]{:S(2)}) async-start(), calls=%async_computation.7 | async-start | bytes 2654208 | tf_op jit(solution)/shard_map/all_gather | solution.py:176
  86.2 79.6 %collective-permute-start.6 = (bf16[256,1024]{1,0:T(8,128)(2,1)}, bf16[256,1024]{1,0:T(8,128)(2,1)}, u32[]{:S(2)}, u32[]{:S(2)}) collective-permute-start(bf16[256,1024]{1,0:T(8,128)(2,1)} %bitcast.33), channel_id=1, source_target_pairs={{0,8},{4,12},{8,0},{12,4},{1,9},{5,13},{9,1},{13,5},{2,10},{6,14},... | collective-permute-start | bytes 1572872 | tf_op jit(solution)/shard_map/ppermute | solution.py:74
  87.7 326.2 %reduce-scatter.8.cloned.1.call-start = ((), (), s32[]{:S(2)}) async-start(), calls=%async_computation.10 | async-start | bytes 2654208 | tf_op jit(solution)/shard_map/reduce_scatter | solution.py:283
  88.3 13.5 %copy-start.60 = (f32[64]{0:T(128)}, f32[64]{0:T(128)S(1)}, u32[]{:S(2)}) copy-start(f32[64]{0:T(128)S(1)} %convert_element_type.248) | copy-start | bytes 772
  88.7 10.8 %copy-start.62 = (f32[256]{0:T(256)}, f32[256]{0:T(256)S(1)}, u32[]{:S(2)}) copy-start(f32[256]{0:T(256)S(1)} %fusion.84) | copy-start | bytes 3076
  99.6 10.4 %copy-start.17 = (bf16[256,512]{1,0:T(8,128)(2,1)}, bf16[256,512]{1,0:T(8,128)(2,1)S(1)}, u32[]{:S(2)}) copy-start(bf16[256,512]{1,0:T(8,128)(2,1)S(1)} %slice.146) | copy-start | bytes 786436
  101.8 8.3 %copy-start.5 = (f32[256,512]{0,1:T(8,128)}, f32[256,512]{0,1:T(8,128)S(1)}, u32[]{:S(2)}) copy-start(f32[256,512]{0,1:T(8,128)S(1)} %copy.112) | copy-start | bytes 1572868
  102.5 8.4 %copy-start.42 = (f32[256,8]{0,1:T(8,128)}, f32[256,8]{0,1:T(8,128)S(1)}, u32[]{:S(2)}) copy-start(f32[256,8]{0,1:T(8,128)S(1)} %fusion.83) | copy-start | bytes 24580
  110.9 14.1 %collective-permute-start = (bf16[256,1024]{1,0:T(8,128)(2,1)}, bf16[256,1024]{1,0:T(8,128)(2,1)}, u32[]{:S(2)}, u32[]{:S(2)}) collective-permute-start(bf16[256,1024]{1,0:T(8,128)(2,1)} %pad_maximum_fusion.16), channel_id=1, source_target_pairs={{0,8},{4,12},{8,0},{12,4},{1,9},{5,13},{9,1},{13,5},{2,10},{6,14},... | collective-permute-start | bytes 1572872 | tf_op jit(solution)/shard_map/ppermute | solution.py:74
  127.3 12.6 %collective-permute-start.1 = (bf16[512,1024]{1,0:T(8,128)(2,1)}, bf16[512,1024]{1,0:T(8,128)(2,1)}, u32[]{:S(2)}, u32[]{:S(2)}) collective-permute-start(bf16[512,1024]{1,0:T(8,128)(2,1)} %pad_maximum_fusion.8), channel_id=1, source_target_pairs={{0,4},{4,0},{8,12},{12,8},{1,5},{5,1},{9,13},{13,9},{2,6},{6,2},{1... | collective-permute-start | bytes 3145736 | tf_op jit(solution)/shard_map/ppermute | solution.py:74
  161.5 18.6 %copy-start.19 = (bf16[256,8,2,64]{0,3,2,1:T(8,128)(2,1)}, bf16[256,8,2,64]{0,3,2,1:T(8,128)(2,1)S(1)}, u32[]{:S(2)}) copy-start(bf16[256,8,2,64]{0,3,2,1:T(8,128)(2,1)S(1)} %get-tuple-element.93) | copy-start | bytes 1572868
  164.2 16.0 %copy-start.58 = (f32[256]{0:T(256)}, f32[256]{0:T(256)S(1)}, u32[]{:S(2)}) copy-start(f32[256]{0:T(256)S(1)} %get-tuple-element.95) | copy-start | bytes 3076
  164.7 14.3 %copy-start.22 = (bf16[256,1024]{1,0:T(8,128)(2,1)}, bf16[256,1024]{1,0:T(8,128)(2,1)S(1)}, u32[]{:S(2)}) copy-start(bf16[256,1024]{1,0:T(8,128)(2,1)S(1)} %multiply_convert_fusion.3) | copy-start | bytes 1572868
  164.7 14.3 %collective-permute-start.2 = (bf16[256,1024]{1,0:T(8,128)(2,1)S(1)}, bf16[256,1024]{1,0:T(8,128)(2,1)S(1)}, u32[]{:S(2)}, u32[]{:S(2)}) collective-permute-start(bf16[256,1024]{1,0:T(8,128)(2,1)S(1)} %multiply_convert_fusion.3), channel_id=1, source_target_pairs={{0,8},{4,12},{8,0},{12,4},{1,9},{5,13},{9,1},{13,5},{2,10},{6,14},... | collective-permute-start | bytes 1572872 | tf_op jit(solution)/shard_map/ppermute | solution.py:74
  168.1 12.2 %collective-permute-start.7 = (bf16[512,1024]{1,0:T(8,128)(2,1)}, bf16[512,1024]{1,0:T(8,128)(2,1)}, u32[]{:S(2)}, u32[]{:S(2)}) collective-permute-start(bf16[512,1024]{1,0:T(8,128)(2,1)} %pad_maximum_fusion.11), channel_id=1, source_target_pairs={{0,4},{4,0},{8,12},{12,8},{1,5},{5,1},{9,13},{13,9},{2,6},{6,2},{1... | collective-permute-start | bytes 3145736 | tf_op jit(solution)/shard_map/ppermute | solution.py:74
  180.2 3.7 collective-permute-start.3
  219.0 10.8 %copy-start.68 = (bf16[1152,1024]{1,0:T(8,128)(2,1)S(1)}, bf16[1152,1024]{1,0:T(8,128)(2,1)}, u32[]{:S(2)}) copy-start(bf16[1152,1024]{1,0:T(8,128)(2,1)} %all-gather.8.cloned.1.call-done) | copy-start | bytes 7077892
  235.3 28.4 %collective-permute-start.4 = (bf16[512,1024]{1,0:T(8,128)(2,1)}, bf16[512,1024]{1,0:T(8,128)(2,1)}, u32[]{:S(2)}, u32[]{:S(2)}) collective-permute-start(bf16[512,1024]{1,0:T(8,128)(2,1)} %pad_maximum_fusion.10), channel_id=1, source_target_pairs={{0,4},{4,0},{8,12},{12,8},{1,5},{5,1},{9,13},{13,9},{2,6},{6,2},{1... | collective-permute-start | bytes 3145736 | tf_op jit(solution)/shard_map/ppermute | solution.py:74
  240.4 10.4 %copy-start.24 = (f32[1024,1024]{1,0:T(8,128)}, f32[1024,1024]{1,0:T(8,128)S(1)}, u32[]{:S(2)}) copy-start(f32[1024,1024]{1,0:T(8,128)S(1)} %get-tuple-element.98) | copy-start | bytes 12582916
  240.6 12.8 %copy-start.34 = (bf16[256,1024]{1,0:T(8,128)(2,1)S(1)}, bf16[256,1024]{1,0:T(8,128)(2,1)}, u32[]{:S(2)}) copy-start(bf16[256,1024]{1,0:T(8,128)(2,1)} %get-tuple-element.67) | copy-start | bytes 1572868
  240.6 12.8 %copy-start.35 = (bf16[256,1024]{1,0:T(8,128)(2,1)S(1)}, bf16[256,1024]{1,0:T(8,128)(2,1)}, u32[]{:S(2)}) copy-start(bf16[256,1024]{1,0:T(8,128)(2,1)} %get-tuple-element.68) | copy-start | bytes 1572868
  240.6 10.1 %collective-permute-start.8 = (bf16[512,1024]{1,0:T(8,128)(2,1)S(1)}, bf16[512,1024]{1,0:T(8,128)(2,1)S(1)}, u32[]{:S(2)}, u32[]{:S(2)}) collective-permute-start(bf16[512,1024]{1,0:T(8,128)(2,1)S(1)} %pad_maximum_fusion.12), channel_id=1, source_target_pairs={{0,4},{4,0},{8,12},{12,8},{1,5},{5,1},{9,13},{13,9},{2,6},{6,2},{1... | collective-permute-start | bytes 3145736 | tf_op jit(solution)/shard_map/ppermute | solution.py:74
  251.9 14.7 %collective-permute-start.9 = (bf16[256,1024]{1,0:T(8,128)(2,1)}, bf16[256,1024]{1,0:T(8,128)(2,1)}, u32[]{:S(2)}, u32[]{:S(2)}) collective-permute-start(bf16[256,1024]{1,0:T(8,128)(2,1)} %fusion.62), channel_id=1, source_target_pairs={{0,8},{4,12},{8,0},{12,4},{1,9},{5,13},{9,1},{13,5},{2,10},{6,14},... | collective-permute-start | bytes 1572872 | tf_op jit(solution)/shard_map/ppermute | solution.py:74
  258.7 7.9 %copy-start.29 = (bf16[512,1024]{1,0:T(8,128)(2,1)S(1)}, bf16[512,1024]{1,0:T(8,128)(2,1)}, u32[]{:S(2)}) copy-start(bf16[512,1024]{1,0:T(8,128)(2,1)} %copy-done.28) | copy-start | bytes 3145732
  266.0 14.3 %collective-permute-start.5 = (bf16[256,1024]{1,0:T(8,128)(2,1)}, bf16[256,1024]{1,0:T(8,128)(2,1)S(1)}, u32[]{:S(2)}, u32[]{:S(2)}) collective-permute-start(bf16[256,1024]{1,0:T(8,128)(2,1)} %fusion.64), channel_id=1, source_target_pairs={{0,8},{4,12},{8,0},{12,4},{1,9},{5,13},{9,1},{13,5},{2,10},{6,14},... | collective-permute-start | bytes 1572872 | tf_op jit(solution)/shard_map/ppermute | solution.py:74
  269.2 187.2 %reduce-scatter.6.cloned.1.call-start = ((), (), s32[]{:S(2)}) async-start(), calls=%async_computation.9 | async-start | bytes 5308416 | tf_op jit(solution)/shard_map/reduce_scatter | solution.py:286
  283.4 7.1 %copy-start.26 = (bf16[1024,512]{0,1:T(8,128)(2,1)S(1)}, bf16[1024,512]{0,1:T(8,128)(2,1)}, u32[]{:S(2)}) copy-start(bf16[1024,512]{0,1:T(8,128)(2,1)} %copy.122) | copy-start | bytes 3145732
  288.8 10.6 %copy-start.20 = (bf16[256,1024]{0,1:T(8,128)(2,1)}, bf16[256,1024]{0,1:T(8,128)(2,1)S(1)}, u32[]{:S(2)}) copy-start(bf16[256,1024]{0,1:T(8,128)(2,1)S(1)} %copy.126) | copy-start | bytes 1572868
  305.3 23.8 %copy-start.3 = (f32[1024,512]{1,0:T(8,128)}, f32[1024,512]{1,0:T(8,128)S(1)}, u32[]{:S(2)}) copy-start(f32[1024,512]{1,0:T(8,128)S(1)} %copy.131) | copy-start | bytes 6291460
  305.3 6.9 %copy-start.21 = (bf16[256,1024]{0,1:T(8,128)(2,1)S(1)}, bf16[256,1024]{0,1:T(8,128)(2,1)}, u32[]{:S(2)}) copy-start(bf16[256,1024]{0,1:T(8,128)(2,1)} %copy-done.20) | copy-start | bytes 1572868
  305.4 6.9 %copy-start.53 = (f32[8,2,256]{2,1,0:T(2,128)S(1)}, f32[8,2,256]{2,1,0:T(2,128)}, u32[]{:S(2)}) copy-start(f32[8,2,256]{2,1,0:T(2,128)} %log_add_fusion) | copy-start | bytes 49156
  326.4 2.7 collective-permute-start.10
  330.2 14.3 %collective-permute-start.11 = (bf16[256,1024]{1,0:T(8,128)(2,1)}, bf16[256,1024]{1,0:T(8,128)(2,1)}, u32[]{:S(2)}, u32[]{:S(2)}) collective-permute-start(bf16[256,1024]{1,0:T(8,128)(2,1)} %fusion.61), channel_id=1, source_target_pairs={{0,8},{4,12},{8,0},{12,4},{1,9},{5,13},{9,1},{13,5},{2,10},{6,14},... | collective-permute-start | bytes 1572872 | tf_op jit(solution)/shard_map/ppermute | solution.py:74
  332.1 171.0 %reduce-scatter.4.cloned.1.call-start = ((), (), s32[]{:S(2)}) async-start(), calls=%async_computation.8 | async-start | bytes 1769472 | tf_op jit(solution)/shard_map/reduce_scatter | solution.py:368
  334.1 14.4 %copy-start.6 = (f32[256,512]{0,1:T(8,128)S(1)}, f32[256,512]{0,1:T(8,128)}, u32[]{:S(2)}) copy-start(f32[256,512]{0,1:T(8,128)} %copy-done.5) | copy-start | bytes 1572868
  334.1 14.4 %copy-start.43 = (f32[256,8]{0,1:T(8,128)S(1)}, f32[256,8]{0,1:T(8,128)}, u32[]{:S(2)}) copy-start(f32[256,8]{0,1:T(8,128)} %copy-done.42) | copy-start | bytes 24580
  363.5 6.0 %collective-permute-start.12 = (bf16[4,128,3072]{2,1,0:T(8,128)(2,1)}, bf16[4,128,3072]{2,1,0:T(8,128)(2,1)}, u32[]{:S(2)}, u32[]{:S(2)}) collective-permute-start(bf16[4,128,3072]{2,1,0:T(8,128)(2,1)} %pad_maximum_fusion.2), channel_id=1, source_target_pairs={{0,4},{4,0},{8,12},{12,8},{1,5},{5,1},{9,13},{13,9},{2,6},{6,2},{1... | collective-permute-start | bytes 9437192 | tf_op jit(solution)/shard_map/ppermute | solution.py:74
  373.1 36.7 %collective-permute-start.13 = (bf16[2,128,3072]{2,1,0:T(8,128)(2,1)}, bf16[2,128,3072]{2,1,0:T(8,128)(2,1)}, u32[]{:S(2)}, u32[]{:S(2)}) collective-permute-start(bf16[2,128,3072]{2,1,0:T(8,128)(2,1)} %fusion.21), channel_id=1, source_target_pairs={{0,8},{4,12},{8,0},{12,4},{1,9},{5,13},{9,1},{13,5},{2,10},{6,14},... | collective-permute-start | bytes 4718600 | tf_op jit(solution)/shard_map/ppermute | solution.py:74
  373.5 42.3 %copy-start.52 = (f32[1024]{0:T(1024)S(1)}, f32[1024]{0:T(1024)}, u32[]{:S(2)}) copy-start(f32[1024]{0:T(1024)} %get-tuple-element.30) | copy-start | bytes 12292
  373.5 42.3 %copy-start.64 = (f32[64]{0:T(128)S(1)}, f32[64]{0:T(128)}, u32[]{:S(2)}) copy-start(f32[64]{0:T(128)} %get-tuple-element.28) | copy-start | bytes 772
  456.4 49.7 %all-to-all-start.1 = ((bf16[4,32,2304]{2,1,0:T(8,128)(2,1)}), bf16[4,32,2304]{2,1,0:T(8,128)(2,1)S(1)}, u32[]{:S(2)}, u32[]{:S(2)}) async-start(bf16[4,32,2304]{2,1,0:T(8,128)(2,1)} %bitcast.215), calls=%async_computation.3 | async-start | bytes 1179648 | tf_op jit(solution)/shard_map/all_to_all | solution.py:287
  (43 other events, 136.5 us)
Sparse Core Ops, SparseCore 0:
  11.4 74.6 all-gather.3
  88.2 78.3 all-gather.5
  168.7 50.2 all-gather.7
  269.4 67.5 reduce-scatter.7
  340.4 94.4 reduce-scatter.5
  438.2 64.8 reduce-scatter.3
